TPU v7x, 128 devices: a whole 4x4x4 slice. The times are simulated.
128 devices in a mesh: dp: 4 (over x), ctx: 32 (over y, z, core).
Axes of the slice: x: 4, y: 4, z: 4, core: 2. Of those that a mesh axis runs over, the one named last changes fastest.
Arguments:
- query_states: bfloat16 [4, 4096, 2048], P('dp', 'ctx'), may hold values from -24 to 24
- key_states: bfloat16 [4, 4096, 1024], P('dp', 'ctx'), may hold values from -6 to 6
- value_states: bfloat16 [4, 4096, 1024], P('dp', 'ctx'), may hold values from -6 to 6
- out_grads: bfloat16 [4, 4096, 2048], P('dp', 'ctx'), may hold values from -6 to 6
- image_counts: int32 [4], P('dp'), may hold values from 256 to 2048, as said below
- prefix_lengths: int32 [4], P('dp'), may hold values from 257 to 3072, as said below
- encoder_owner: int32 [4], replicated, may hold values from 0 to 3, each once
- key_weight: bfloat16 [4608, 1024], replicated, may hold values from -0.09375 to 0.09375
- value_weight: bfloat16 [4608, 1024], replicated, may hold values from -0.09375 to 0.09375
- norm_scale: float32 [4608], P('dp'), may hold values from 0.5 to 2
- image_embed: bfloat16 [4, 2048, 4608], P(None, 'ctx', 'dp'), may hold values from -1200 to 1200
Outputs:
- query_grads: bfloat16 [4, 4096, 2048], P('dp', 'ctx')
- key_grads: bfloat16 [4, 4096, 1024], P('dp', 'ctx')
- value_grads: bfloat16 [4, 4096, 1024], P('dp', 'ctx')
- image_grads: float32 [4, 2048, 4608], P(None, 'ctx', 'dp')
Inputs may be any that keep to these rules, and one draw needn't show every extreme that they name: `image_counts`: in every draw one sample has exactly 2048 image tokens and another exactly 256. `prefix_lengths`: each is at least one more than its sample's image_counts; in every draw one reaches 3072.
All inputs are finite; a program needn't handle non-finite values.
Results may differ from a plain program's by a relative error of at most 0.02.
Values may be sent and summed in bfloat16 or wider, within the bound.
No kernel may reach another device: no remote copies, remote signals or barrier semaphores. Data moves between devices by JAX's collectives and lax.ppermute only.
A program may use at most 192 MiB of HBM per device.

v0:
```python
import jax
import jax.numpy as jnp
from jax import lax
from jax.sharding import PartitionSpec as P

D = 4608
HD = 128


score_scale = 144.0 ** (-0.5)
soft_cap = 50.0
norm_eps = 1e-06
block_rows = 512


def visibility(query_pos, key_pos, prefix):
    return (key_pos[None, :] < prefix) | (key_pos[None, :] <= query_pos[:, None])


def capped_scores(query_four, key_block, head_size):
    key_heads = key_block.reshape(key_block.shape[0], -1, head_size)
    raw_scores = (
        jnp.einsum("qgmd,kgd->gmqk", query_four, key_heads, preferred_element_type=jnp.float32)
        * score_scale
    )
    squashed = jnp.tanh(raw_scores / soft_cap)
    return (squashed, soft_cap * squashed)


def value_scores(grad_four, value_block, head_size):
    value_heads = value_block.reshape(value_block.shape[0], -1, head_size)
    return jnp.einsum("qgmd,kgd->gmqk", grad_four, value_heads, preferred_element_type=jnp.float32)


def key_steps_of(key_all, value_all):
    seq_len = key_all.shape[0]
    step_rows = min(block_rows, seq_len)
    n_steps = seq_len // step_rows
    key_steps = key_all.reshape(n_steps, step_rows, key_all.shape[1])
    value_steps = value_all.reshape(n_steps, step_rows, value_all.shape[1])
    starts = jnp.arange(n_steps) * step_rows
    return (key_steps, value_steps, starts, step_rows)


def row_stats(query_four, grad_four, key_all, value_all, query_pos, prefix, head_size):
    key_steps, value_steps, starts, step_rows = key_steps_of(key_all, value_all)

    def stats_step(carry, inputs):
        totals, moments = carry
        key_block, value_block, offset = inputs
        squashed, capped = capped_scores(query_four, key_block, head_size)
        visible = visibility(query_pos, offset + jnp.arange(step_rows), prefix)
        unnormed = jnp.where(visible, jnp.exp(capped), 0.0)
        prob_grads = value_scores(grad_four, value_block, head_size)
        return (
            (totals + jnp.sum(unnormed, -1), moments + jnp.sum(unnormed * prob_grads, -1)),
            None,
        )

    stat_zero = jnp.zeros(
        (query_four.shape[1], query_four.shape[2], query_four.shape[0]), jnp.float32
    )
    (totals, moments), _ = lax.scan(
        stats_step, (stat_zero, stat_zero), (key_steps, value_steps, starts)
    )
    return (jnp.log(totals), moments / totals)


def grads_block(
    query_four,
    grad_four,
    key_block,
    value_block,
    offset,
    query_pos,
    prefix,
    log_total,
    row_delta,
    head_size,
):
    squashed, capped = capped_scores(query_four, key_block, head_size)
    visible = visibility(query_pos, offset + jnp.arange(key_block.shape[0]), prefix)
    soft_probs = jnp.where(visible, jnp.exp(capped - log_total[..., None]), 0.0)
    prob_grads = value_scores(grad_four, value_block, head_size)
    weight_grad = (
        score_scale * soft_probs * (prob_grads - row_delta[..., None]) * (1.0 - squashed * squashed)
    ).astype(jnp.bfloat16)
    return (weight_grad, soft_probs.astype(jnp.bfloat16))


def query_term(weight_grad, key_block, head_size):
    key_heads = key_block.reshape(key_block.shape[0], -1, head_size)
    return jnp.einsum("gmqk,kgd->qgmd", weight_grad, key_heads, preferred_element_type=jnp.float32)


def key_term(weight_grad, probs_bf, query_four, grad_four, query_blocks):
    kv_heads, group_size, rows, count = weight_grad.shape
    block_len = rows // query_blocks
    head_size = query_four.shape[3]
    weight_split = weight_grad.reshape(kv_heads, group_size, query_blocks, block_len, count)
    probs_split = probs_bf.reshape(kv_heads, group_size, query_blocks, block_len, count)
    query_split = query_four.reshape(query_blocks, block_len, kv_heads, group_size, head_size)
    grad_split = grad_four.reshape(query_blocks, block_len, kv_heads, group_size, head_size)
    key_part = jnp.einsum(
        "gmnqk,nqgmd->nkgd", weight_split, query_split, preferred_element_type=jnp.float32
    ).astype(jnp.bfloat16)
    value_part = jnp.einsum(
        "gmnqk,nqgmd->nkgd", probs_split, grad_split, preferred_element_type=jnp.float32
    ).astype(jnp.bfloat16)
    key_sum = jnp.sum(key_part.astype(jnp.float32), 0).reshape(count, kv_heads * head_size)
    value_sum = jnp.sum(value_part.astype(jnp.float32), 0).reshape(count, kv_heads * head_size)
    return (key_sum, value_sum)


def sweep(
    query_four,
    grad_four,
    key_all,
    value_all,
    query_pos,
    prefix,
    log_total,
    row_delta,
    head_size,
    query_blocks,
):
    key_steps, value_steps, starts, step_rows = key_steps_of(key_all, value_all)

    def grad_step(query_acc, inputs):
        key_block, value_block, offset = inputs
        weight_grad, probs_bf = grads_block(
            query_four,
            grad_four,
            key_block,
            value_block,
            offset,
            query_pos,
            prefix,
            log_total,
            row_delta,
            head_size,
        )
        query_acc = query_acc + query_term(weight_grad, key_block, head_size)
        return (query_acc, key_term(weight_grad, probs_bf, query_four, grad_four, query_blocks))

    query_zero = jnp.zeros(query_four.shape, jnp.float32)
    query_acc, (key_parts, value_parts) = lax.scan(
        grad_step, query_zero, (key_steps, value_steps, starts)
    )
    seq_len = key_all.shape[0]
    return (query_acc, key_parts.reshape(seq_len, -1), value_parts.reshape(seq_len, -1))


def local(
    query_states,
    key_states,
    value_states,
    out_grads,
    image_counts,
    prefix_lengths,
    encoder_owner,
    key_weight,
    value_weight,
    norm_scale,
    image_embed,
):
    head_size = HD
    queries = query_states[0]
    tok_rows = queries.shape[0]
    query_width = queries.shape[1]
    kv_width = key_states.shape[2]
    kv_heads = kv_width // head_size
    group_size = query_width // kv_width
    ctx_size = lax.axis_size("ctx")
    ctx_rank = lax.axis_index("ctx")
    prefix = prefix_lengths[0]
    query_four = queries.reshape(tok_rows, kv_heads, group_size, head_size)
    grad_four = out_grads[0].reshape(tok_rows, kv_heads, group_size, head_size)
    query_pos = ctx_rank * tok_rows + jnp.arange(tok_rows)
    key_all, value_all = (
        lax.all_gather(key_states[0], "ctx", axis=0, tiled=True),
        lax.all_gather(value_states[0], "ctx", axis=0, tiled=True),
    )
    log_total, row_delta = row_stats(
        query_four, grad_four, key_all, value_all, query_pos, prefix, head_size
    )
    query_acc, key_part, value_part = sweep(
        query_four,
        grad_four,
        key_all,
        value_all,
        query_pos,
        prefix,
        log_total,
        row_delta,
        head_size,
        1,
    )
    key_sum, value_sum = (
        lax.psum_scatter(
            key_part.astype(jnp.bfloat16), "ctx", scatter_dimension=0, tiled=True
        ).astype(jnp.float32),
        lax.psum_scatter(
            value_part.astype(jnp.bfloat16), "ctx", scatter_dimension=0, tiled=True
        ).astype(jnp.float32),
    )
    query_grads = query_acc.reshape(tok_rows, query_width).astype(jnp.bfloat16)
    key_grads = key_sum.astype(jnp.bfloat16)
    value_grads = value_sum.astype(jnp.bfloat16)
    dp_size = lax.axis_size("dp")
    own_pos = ctx_rank * tok_rows + jnp.arange(tok_rows)
    is_image = (own_pos < image_counts[0])[:, None]
    projected = jnp.einsum("tk,dk->td", key_grads, key_weight, preferred_element_type=jnp.float32)
    projected = projected + jnp.einsum(
        "tk,dk->td", value_grads, value_weight, preferred_element_type=jnp.float32
    )
    payload = jnp.where(is_image, projected, 0.0).astype(jnp.bfloat16)
    share = payload.shape[1] // dp_size
    per_peer = tok_rows // ctx_size
    outgoing = payload.reshape(per_peer, ctx_size, dp_size, share)
    arrived_rows = lax.all_to_all(
        lax.all_to_all(outgoing, "dp", split_axis=2, concat_axis=2, tiled=True),
        "ctx",
        split_axis=1,
        concat_axis=1,
        tiled=True,
    )
    enc_rows = image_embed.shape[1]
    by_sample = arrived_rows.transpose(2, 1, 0, 3).reshape(dp_size, tok_rows, share)[:, :enc_rows]
    pick = (encoder_owner[:, None] == jnp.arange(dp_size)[None, :]).astype(jnp.bfloat16)
    landed = jnp.einsum("bk,bsf->ksf", pick, by_sample, preferred_element_type=jnp.float32).astype(
        jnp.bfloat16
    )
    embed_rows = image_embed.astype(jnp.float32)
    scaled = norm_scale * landed.astype(jnp.float32)
    square_sum, cross_sum = lax.psum(
        (jnp.sum(embed_rows * embed_rows, -1), jnp.sum(embed_rows * scaled, -1)), "dp"
    )
    inv_rms = lax.rsqrt(square_sum / D + norm_eps)[..., None]
    cross_mean = (cross_sum / D)[..., None]
    image_grads = inv_rms * scaled - embed_rows * (inv_rms * inv_rms * inv_rms) * cross_mean
    return (query_grads[None], key_grads[None], value_grads[None], image_grads)


def solution(mesh):
    in_specs = (
        P("dp", "ctx", None),
        P("dp", "ctx", None),
        P("dp", "ctx", None),
        P("dp", "ctx", None),
        P("dp"),
        P("dp"),
        P(),
        P(),
        P(),
        P("dp"),
        P(None, "ctx", "dp"),
    )
    out_specs = (
        P("dp", "ctx", None),
        P("dp", "ctx", None),
        P("dp", "ctx", None),
        P(None, "ctx", "dp"),
    )
    return jax.shard_map(local, mesh=mesh, in_specs=in_specs, out_specs=out_specs, check_vma=False)
```

profile of v0, /device:TPU:0, one launch (start us, length us, event | category | flops | bytes accessed | tf_op | source)
XLA Modules:
  0.0 655.7 jit_solution(5189165472124397349)
XLA Ops:
  13.4 52.4 %all-gather.5.cloned.1.call-done = bf16[1,4096,1024]{2,1,0:T(8,128)(2,1)} async-done(((bf16[1,128,1024]{2,1,0:T(8,128)(2,1)}), bf16[1,4096,1024]{2,1,0:T(8,128)(2,1)}) %all-gather.5.cloned.1.call-update) | async-done | bytes 8388624 | tf_op jit(solution)/shard_map/all_gather | solution.py:181
  65.8 11.5 %copy.86 = bf16[8,512,1024]{1,2,0:T(8,128)(2,1)} copy(bf16[8,512,1024]{2,1,0:T(8,128)(2,1)} %bitcast.209) | data formatting | bytes 16777216
  77.3 43.3 %all-gather.7.cloned.1.call-done = bf16[1,4096,1024]{2,1,0:T(8,128)(2,1)} async-done(((bf16[1,128,1024]{2,1,0:T(8,128)(2,1)}), bf16[1,4096,1024]{2,1,0:T(8,128)(2,1)}) %all-gather.7.cloned.1.call-update) | async-done | bytes 8388624 | tf_op jit(solution)/shard_map/all_gather | solution.py:182
  120.6 11.4 %copy.84 = bf16[8,512,1024]{1,2,0:T(8,128)(2,1)} copy(bf16[8,512,1024]{2,1,0:T(8,128)(2,1)} %bitcast.210) | data formatting | bytes 16777216
  132.0 84.2 %while.32 = (s32[]{:T(128)}, f32[8,2,128]{2,1,0:T(2,128)S(1)}, f32[8,2,128]{2,1,0:T(2,128)S(1)}, s32[8]{0:T(128)S(1)}, s32[]{:T(128)}, /*index=5*/bf16[8,512,102...) while((s32[]{:T(128)}, f32[8,2,128]{2,1,0:T(2,128)S(1)}, ...), condition=%wide.region_3.4_spmd.clone, body=%wide.region_0.3_spmd.clone.sunk | while | flops 546444928 | bytes 15997099 | solution.py:63
  216.3 161.2 %while.33 = (s32[]{:T(128)}, f32[128,8,2,128]{0,3,2,1:T(8,128)}, bf16[8,512,1024]{1,2,0:T(8,128)(2,1)}, bf16[8,512,1024]{1,2,0:T(8,128)(2,1)}, bf16[8,512,1024]{...) while((s32[]{:T(128)}, f32[128,8,2,128]{0,3,2,1:T(8,128)}, ...), condition=%wide.region_5.6_spmd.clone, body=%wide.region_4.5_spmd.clone.sunk | while | flops 1360660096 | bytes 78870904 | solution.py:147
  225.3 3.5 fusion.98
  245.1 3.5 fusion.98
  265.3 3.5 fusion.98
  285.5 3.5 fusion.98
  305.7 3.5 fusion.98
  325.8 3.5 fusion.98
  346.0 3.5 fusion.98
  366.2 3.5 fusion.98
  377.4 11.5 %copy.93 = bf16[8,512,1024]{2,1,0:T(8,128)(2,1)} copy(bf16[8,512,1024]{1,2,0:T(8,128)(2,1)} %get-tuple-element.320) | data formatting | bytes 16777216 | tf_op jit(solution)/shard_map/convert_element_type | solution.py:201
  389.2 11.5 %copy.94 = bf16[8,512,1024]{2,1,0:T(8,128)(2,1)} copy(bf16[8,512,1024]{1,2,0:T(8,128)(2,1)} %get-tuple-element.321) | data formatting | bytes 16777216 | tf_op jit(solution)/shard_map/convert_element_type | solution.py:204
  401.4 80.1 %reduce-scatter.3.cloned.1.call-done = bf16[128,1024]{1,0:T(8,128)(2,1)} async-done(((bf16[4096,1024]{1,0:T(8,128)(2,1)}), bf16[128,1024]{1,0:T(8,128)(2,1)}) %reduce-scatter.3.cloned.1.call-update) | async-done | bytes 262160 | tf_op jit(solution)/shard_map/reduce_scatter | solution.py:200
  481.5 7.0 %fusion.42 = f32[128,4608]{1,0:T(8,128)S(1)} fusion(bf16[128,1024]{1,0:T(8,128)(2,1)} %reduce-scatter.3.cloned.1.call-done, bf16[4608,1024]{1,0:T(8,128)(2,1)} %param.22), kind=kOutput, calls=%fused_computation.70 | convolution fusion | flops 1207959552 | bytes 12058624 | tf_op jit(solution)/shard_map/tk,dk->td/dot_general | solution.py:213
  488.5 89.7 %reduce-scatter.5.cloned.1.call-done = bf16[128,1024]{1,0:T(8,128)(2,1)} async-done(((bf16[4096,1024]{1,0:T(8,128)(2,1)}), bf16[128,1024]{1,0:T(8,128)(2,1)}) %reduce-scatter.5.cloned.1.call-update) | async-done | bytes 262160 | tf_op jit(solution)/shard_map/reduce_scatter | solution.py:203
  578.2 7.0 %fusion.29 = bf16[128,4608]{1,0:T(8,128)(2,1)S(1)} fusion(f32[128,4608]{1,0:T(8,128)S(1)} %fusion.42, bf16[128,1024]{1,0:T(8,128)(2,1)} %reduce-scatter.5.cloned.1.call-done, bf16[4608,1024]{1,0:T(8,128)(2,1)} %param.23, pred[128]{0:T(512)(128)(4,1)S(1)} %add_compare_fusion), kind=kOutput, calls=%fused_computation.48 | convolution fusion | flops 1209729024 | bytes 13238400 | tf_op jit(solution)/shard_map/tk,dk->td/dot_general | solution.py:214
  585.7 19.0 %all_to_all.10 = bf16[4,32,4,1152]{3,1,0,2:T(8,128)(2,1)S(1)} all-to-all(bf16[4,32,4,1152]{3,1,0,2:T(8,128)(2,1)S(1)} %copy.96), channel_id=1, replica_groups=mesh['dp'=4,'ctx'=32] {'dp'}, dimensions={2} | all-to-all | bytes 2359296 | tf_op jit(solution)/shard_map/all_to_all | solution.py:222
  606.7 5.3 all-to-all-start.1
  613.1 17.3 %all-to-all-done.1 = bf16[4,32,4,1152]{3,2,0,1:T(4,128)(2,1)S(1)} async-done(((bf16[4,32,4,1152]{3,2,0,1:T(4,128)(2,1)}), bf16[4,32,4,1152]{3,2,0,1:T(4,128)(2,1)S(1)}, u32[]{:S(2)}, u32[]{:S(2)}) %all-to-all-start.1) | async-done | bytes 1179680 | tf_op jit(solution)/shard_map/all_to_all | solution.py:221
  631.4 16.0 %all-reduce = (f32[4,64]{0,1:T(8,128)S(1)}, f32[4,64]{0,1:T(8,128)S(1)}) all-reduce(f32[4,64]{0,1:T(8,128)S(1)} %get-tuple-element.516, f32[4,64]{0,1:T(8,128)S(1)} %get-tuple-element.515), channel_id=1, replica_groups=mesh['dp'=4,'ctx'=32] {'dp'}, use_global_device_ids=true, to_apply=%region_11.12 | all-reduce | flops 512 | bytes 4096 | tf_op jit(solution)/shard_map/psum | solution.py:236
  (309 shorter events, 228.5 us)
Async XLA Ops:
  7.2 58.6 %all-gather.5.cloned.1.call-start = ((), (), s32[]{:S(2)}) async-start(), calls=%async_computation.6 | async-start | bytes 8650752 | tf_op jit(solution)/shard_map/all_gather | solution.py:181
  7.9 112.7 %all-gather.7.cloned.1.call-start = ((), (), s32[]{:S(2)}) async-start(), calls=%async_computation.7 | async-start | bytes 8650752 | tf_op jit(solution)/shard_map/all_gather | solution.py:182
  8.6 472.9 %reduce-scatter.3.cloned.1.call-start = ((), (), s32[]{:S(2)}) async-start(), calls=%async_computation.4 | async-start | bytes 8650752 | tf_op jit(solution)/shard_map/reduce_scatter | solution.py:200
  220.4 8.4 %copy-start = (f32[8,512,128,2]{2,1,3,0:T(8,128)}, f32[8,512,128,2]{2,1,3,0:T(8,128)S(1)}, u32[]{:S(2)}) copy-start(f32[8,512,128,2]{2,1,3,0:T(8,128)S(1)} %fusion.97) | copy-start | bytes 12582916 | tf_op jit(solution)/shard_map/while
  240.2 8.4 %copy-start = (f32[8,512,128,2]{2,1,3,0:T(8,128)}, f32[8,512,128,2]{2,1,3,0:T(8,128)S(1)}, u32[]{:S(2)}) copy-start(f32[8,512,128,2]{2,1,3,0:T(8,128)S(1)} %fusion.97) | copy-start | bytes 12582916 | tf_op jit(solution)/shard_map/while
  248.6 2.9 copy-start.1
  260.4 8.4 %copy-start = (f32[8,512,128,2]{2,1,3,0:T(8,128)}, f32[8,512,128,2]{2,1,3,0:T(8,128)S(1)}, u32[]{:S(2)}) copy-start(f32[8,512,128,2]{2,1,3,0:T(8,128)S(1)} %fusion.97) | copy-start | bytes 12582916 | tf_op jit(solution)/shard_map/while
  268.8 2.9 copy-start.1
  280.6 8.4 %copy-start = (f32[8,512,128,2]{2,1,3,0:T(8,128)}, f32[8,512,128,2]{2,1,3,0:T(8,128)S(1)}, u32[]{:S(2)}) copy-start(f32[8,512,128,2]{2,1,3,0:T(8,128)S(1)} %fusion.97) | copy-start | bytes 12582916 | tf_op jit(solution)/shard_map/while
  289.0 2.9 copy-start.1
  300.8 8.4 %copy-start = (f32[8,512,128,2]{2,1,3,0:T(8,128)}, f32[8,512,128,2]{2,1,3,0:T(8,128)S(1)}, u32[]{:S(2)}) copy-start(f32[8,512,128,2]{2,1,3,0:T(8,128)S(1)} %fusion.97) | copy-start | bytes 12582916 | tf_op jit(solution)/shard_map/while
  309.2 2.9 copy-start.1
  321.0 8.4 %copy-start = (f32[8,512,128,2]{2,1,3,0:T(8,128)}, f32[8,512,128,2]{2,1,3,0:T(8,128)S(1)}, u32[]{:S(2)}) copy-start(f32[8,512,128,2]{2,1,3,0:T(8,128)S(1)} %fusion.97) | copy-start | bytes 12582916 | tf_op jit(solution)/shard_map/while
  329.4 2.9 copy-start.1
  341.2 8.4 %copy-start = (f32[8,512,128,2]{2,1,3,0:T(8,128)}, f32[8,512,128,2]{2,1,3,0:T(8,128)S(1)}, u32[]{:S(2)}) copy-start(f32[8,512,128,2]{2,1,3,0:T(8,128)S(1)} %fusion.97) | copy-start | bytes 12582916 | tf_op jit(solution)/shard_map/while
  349.6 2.9 copy-start.1
  361.3 8.4 %copy-start = (f32[8,512,128,2]{2,1,3,0:T(8,128)}, f32[8,512,128,2]{2,1,3,0:T(8,128)S(1)}, u32[]{:S(2)}) copy-start(f32[8,512,128,2]{2,1,3,0:T(8,128)S(1)} %fusion.97) | copy-start | bytes 12582916 | tf_op jit(solution)/shard_map/while
  369.8 2.9 copy-start.1
  389.0 189.2 %reduce-scatter.5.cloned.1.call-start = ((), (), s32[]{:S(2)}) async-start(), calls=%async_computation.5 | async-start | bytes 8650752 | tf_op jit(solution)/shard_map/reduce_scatter | solution.py:203
  585.6 26.4 %copy-start.2 = (f32[128,8,2,128]{0,3,2,1:T(8,128)S(1)}, f32[128,8,2,128]{0,3,2,1:T(8,128)}, u32[]{:S(2)}) copy-start(f32[128,8,2,128]{0,3,2,1:T(8,128)} %get-tuple-element.319) | copy-start | bytes 3145732
  604.7 25.7 %copy-start.7 = (bf16[4,64,1152]{2,1,0:T(8,128)(2,1)S(1)}, bf16[4,64,1152]{2,1,0:T(8,128)(2,1)}, u32[]{:S(2)}) copy-start(bf16[4,64,1152]{2,1,0:T(8,128)(2,1)} %param.25) | copy-start | bytes 1769476
  604.7 25.7 %copy-start.8 = (f32[1152]{0:T(1024)S(1)}, f32[1152]{0:T(1024)}, u32[]{:S(2)}) copy-start(f32[1152]{0:T(1024)} %param.24) | copy-start | bytes 13828
  604.7 25.7 %copy-start.9 = (s32[4]{0:T(128)S(1)}, s32[4]{0:T(128)}, u32[]{:S(2)}) copy-start(s32[4]{0:T(128)} %param.21) | copy-start | bytes 52
  606.7 23.7 %all-to-all-start.1 = ((bf16[4,32,4,1152]{3,2,0,1:T(4,128)(2,1)}), bf16[4,32,4,1152]{3,2,0,1:T(4,128)(2,1)S(1)}, u32[]{:S(2)}, u32[]{:S(2)}) async-start(bf16[4,32,4,1152]{3,2,0,1:T(4,128)(2,1)} %copy.97), calls=%async_computation.3 | async-start | bytes 2359296 | tf_op jit(solution)/shard_map/all_to_all | solution.py:221
  (33 other events, 55.4 us)
Sparse Core Ops, SparseCore 0:
  10.3 55.4 all-gather.4
  68.0 52.5 all-gather.6
  389.1 92.3 reduce-scatter.2
  486.1 92.0 reduce-scatter.4
where the time goes:
time: 661 us; the launch traced here: 656 us
  waiting for transfers between devices  284 us (43%)
  matrix products  146 us (22%)
  local copies, waits for them, and re-layouts  133 us (20%)
  other arithmetic  35.3 us (5%)
  blocking collectives  35 us (5%)
  between operations  14.6 us (2%)
    reduce_scatter x1, waiting for transfers between devices, local(): lax.psum_scatter(value_part.astype(jnp.bfloat16), 'ctx', scatter_dimensio...  89.7 us
    reduce_scatter x1, waiting for transfers between devices, local(): lax.psum_scatter(key_part.astype(jnp.bfloat16), 'ctx', scatter_dimension=...  80.1 us
    dynamic_slice x48, local copies, waits for them, and re-layouts, row_stats(): lax.scan(stats_step, (stat_zero, stat_zero), (key_steps, value_steps, sta...  57.4 us
    all_gather x1, waiting for transfers between devices, local(): lax.all_gather(key_states[0], 'ctx', axis=0, tiled=True)  52.4 us
    dot_general x16, matrix products, value_scores(): jnp.einsum('qgmd,kgd->gmqk', grad_four, value_heads, preferred_element_ty...  49 us
    all_gather x1, waiting for transfers between devices, local(): lax.all_gather(value_states[0], 'ctx', axis=0, tiled=True)  43.3 us
    dot_general x16, matrix products, capped_scores(): jnp.einsum('qgmd,kgd->gmqk', query_four, key_heads, preferred_element_typ...  34.4 us
    unnamed x15, local copies, waits for them, and re-layouts  28.7 us
  transfers between devices with their start and end apart: 5, of which 5 were waited for; matrix products, arithmetic and copies ran while one was open for 5% of the time, Pallas kernels for 0%

commit v1 on v0

v1 whole, which is shorter than its diff:
```python
import functools
import math

import jax
import jax.numpy as jnp
from jax import lax
from jax.experimental import pallas as pl
from jax.experimental.pallas import tpu as pltpu
from jax.sharding import Mesh, PartitionSpec as P

D = 4608
HD = 128
KVH = 8
TOK = 128
SLOTS = 64
NDP = 4
FS = D // NDP
SEG = 512
NSEG = 8

score_scale = 144.0 ** (-0.5)
soft_cap = 50.0
norm_eps = 1e-06
tanh_scale = score_scale / soft_cap
exp2_scale = soft_cap * math.log2(math.e)

f32 = jnp.float32
bf16 = jnp.bfloat16
VM = pl.BlockSpec(memory_space=pltpu.VMEM)
SM = pl.BlockSpec(memory_space=pltpu.SMEM)
NT = (((1,), (1,)), ((), ()))
NN = (((1,), (0,)), ((), ()))


def mm(a, b, dims=NN):
    return lax.dot_general(a, b, dims, preferred_element_type=f32)


def split3(x):
    hi = x.astype(bf16)
    rest = x - hi.astype(f32)
    mid = rest.astype(bf16)
    lo = (rest - mid.astype(f32)).astype(bf16)
    return hi, mid, lo


def pack_kernel(width, a_ref, b_ref, out_ref):
    for h in range(KVH):
        out_ref[h, :, :width] = a_ref[:, h * width : (h + 1) * width]
        out_ref[h, :, width:] = b_ref[:, h * width : (h + 1) * width]


def pack_heads(a, b, name):
    width = a.shape[1] // KVH
    return pl.pallas_call(
        functools.partial(pack_kernel, width),
        out_shape=jax.ShapeDtypeStruct((KVH, TOK, 2 * width), bf16),
        in_specs=[VM, VM],
        out_specs=VM,
        name=name,
    )(a, b)


def embed_pack_kernel(owner_ref, embed_ref, scale_ref, out_ref):
    out_ref[0, :SLOTS, :] = embed_ref[0]
    row = lax.broadcasted_iota(jnp.int32, (16, FS), 0)
    hi, mid, lo = split3(scale_ref[...])
    parts = jnp.where(row == 0, hi.astype(f32), jnp.where(row == 1, mid.astype(f32), 0.0))
    parts = jnp.where(row == 2, lo.astype(f32), parts)
    out_ref[0, SLOTS:, :] = parts.astype(bf16)


def pack_embed(owner, embed, scale):
    return pl.pallas_call(
        embed_pack_kernel,
        out_shape=jax.ShapeDtypeStruct((NDP, SLOTS + 16, FS), bf16),
        grid_spec=pltpu.PrefetchScalarGridSpec(
            num_scalar_prefetch=1,
            grid=(NDP,),
            in_specs=[
                pl.BlockSpec((1, SLOTS, FS), lambda b, owner: (owner[b], 0, 0)),
                pl.BlockSpec((1, FS), lambda b, owner: (0, 0)),
            ],
            out_specs=pl.BlockSpec((1, SLOTS + 16, FS), lambda b, owner: (b, 0, 0)),
        ),
        name="pack_embed",
    )(owner, embed, scale)


def attention_kernel(
    sc_ref,
    qd_ref,
    kv0_ref,
    kv1_ref,
    kv2_ref,
    kv3_ref,
    dq_ref,
    own_ref,
    core_ref,
    far_ref,
    farcore_ref,
    tok_ref,
    k_s,
    v_s,
    kt_s,
    q_s,
    do_s,
    e_s,
    w_s,
    p_s,
    dk_s,
    dv_s,
    tot,
    mom,
    dqt,
    perm,
):
    prefix, zh, core = sc_ref[0], sc_ref[1], sc_ref[2]
    eye = (
        lax.broadcasted_iota(jnp.int32, (HD, HD), 0) == lax.broadcasted_iota(jnp.int32, (HD, HD), 1)
    ).astype(bf16)
    for seg in range(NSEG):
        near, away = ((kv0_ref, kv1_ref), (kv2_ref, kv3_ref))[seg // 4]
        y = seg % 4
        whole = jnp.concatenate([near[2 * y], near[2 * y + 1], away[2 * y], away[2 * y + 1]], 0)
        k_s[seg] = whole[:, :HD]
        v_s[seg] = whole[:, HD:]
        kt_s[seg] = mm(eye, whole[:, :HD], NT).astype(bf16)
    dk_s[...] = jnp.zeros_like(dk_s)
    dv_s[...] = jnp.zeros_like(dv_s)

    def key_start(j):
        far = j // 4
        return (j % 4) * 1024 + (zh + far - 2 * zh * far) * SEG

    def hidden(key0, row0):
        s = lax.broadcasted_iota(jnp.int32, (SEG, SEG), 0)
        piece = s // TOK
        other = piece // 2
        key = key0 + (piece % 2) * 256 + (core + other - 2 * core * other) * TOK + s % TOK
        lane = lax.broadcasted_iota(jnp.int32, (1, SEG), 1)
        row = row0 + ((lane // TOK) % 2) * 256 + lane % TOK
        return key >= jnp.maximum(row + 1, prefix)

    def row_body(i, _):
        row0 = i * 1024 + zh * SEG + core * TOK
        limit = jnp.maximum(prefix, row0 + 384)
        full = jnp.maximum(prefix, row0 + 1)
        for head in range(2):
            for z in range(2):
                at = pl.ds((head * 2 + z) * TOK, TOK)
                q_s[at, :] = qd_ref[2 * i + z, :, head * HD : (head + 1) * HD]
                do_s[at, :] = qd_ref[2 * i + z, :, (2 + head) * HD : (3 + head) * HD]
        tot[...] = jnp.zeros_like(tot)
        mom[...] = jnp.zeros_like(mom)
        dqt[...] = jnp.zeros_like(dqt)

        def scores(j, key0, masked):
            t = jnp.tanh(mm(k_s[j], q_s[...], NT) * tanh_scale)
            e = jnp.exp2(t * exp2_scale)
            if masked:
                e = jnp.where(hidden(key0, row0), 0.0, e)
            dp = mm(v_s[j], do_s[...], NT)
            tot[...] += jnp.sum(e, 0, keepdims=True)
            mom[...] += jnp.sum(e * dp, 0, keepdims=True)
            e_s[j] = e
            w_s[j] = e * (1.0 - t * t)
            p_s[j] = dp

        def first(j, _):
            key0 = key_start(j)

            @pl.when(key0 + SEG <= full)
            def _():
                scores(j, key0, False)

            @pl.when((key0 + SEG > full) & (key0 < limit))
            def _():
                scores(j, key0, True)

            return 0

        lax.fori_loop(0, NSEG, first, 0)
        inv = 1.0 / tot[...]
        delta = mom[...] * inv

        def second(j, _):
            @pl.when(key_start(j) < limit)
            def _():
                p = (e_s[j] * inv).astype(bf16)
                ds = (w_s[j] * inv * (p_s[j] - delta)).astype(bf16)
                dv_s[j] += mm(p, do_s[...])
                dk_s[j] += mm(ds, q_s[...])
                dqt[...] += mm(kt_s[j], ds)

            return 0

        lax.fori_loop(0, NSEG, second, 0)
        dq = (dqt[...] * score_scale).T.astype(bf16)
        for head in range(2):
            for z in range(2):
                at = (head * 2 + z) * TOK
                dq_ref[2 * i + z, :, head * HD : (head + 1) * HD] = dq[at : at + TOK]
        return 0

    lax.fori_loop(0, 4, row_body, 0)

    out = lax.broadcasted_iota(jnp.int32, (SEG, SEG), 0)
    src = lax.broadcasted_iota(jnp.int32, (SEG, SEG), 1)
    slot = out % 16
    c_of = (slot // 4) % 2
    want = (
        (c_of + core - 2 * c_of * core) * 256 + (slot // 8) * TOK + (slot % 4) * 32 + out // 16
    )
    perm[...] = (want == src).astype(bf16)
    for seg in range(NSEG):
        near, away = ((own_ref, core_ref), (far_ref, farcore_ref))[seg // 4]
        y = seg % 4
        terms = jnp.concatenate([dk_s[seg] * score_scale, dv_s[seg]], 1)
        near[2 * y] = terms[:TOK].astype(near.dtype)
        near[2 * y + 1] = terms[TOK : 2 * TOK].astype(near.dtype)
        away[2 * y] = terms[2 * TOK : 3 * TOK].astype(away.dtype)
        away[2 * y + 1] = terms[3 * TOK :].astype(away.dtype)
        if y < 2:
            moved = mm(perm[...], terms.astype(bf16)).astype(bf16).reshape(32, 16, 2 * HD)
            z_at = zh if seg < 4 else 1 - zh
            tok_ref[:, pl.ds(pl.multiple_of((2 * y + z_at) * 16, 16), 16), :] = moved


def attention(sc, qd, kv0, kv1, kv2, kv3):
    part = (KVH, TOK, 2 * HD)
    return pl.pallas_call(
        attention_kernel,
        out_shape=(
            jax.ShapeDtypeStruct(part, bf16),
            jax.ShapeDtypeStruct(part, f32),
            jax.ShapeDtypeStruct(part, bf16),
            jax.ShapeDtypeStruct(part, bf16),
            jax.ShapeDtypeStruct(part, bf16),
            jax.ShapeDtypeStruct((32, SLOTS, 2 * HD), bf16),
        ),
        in_specs=[SM] + [VM] * 5,
        out_specs=(VM,) * 6,
        scratch_shapes=[
            pltpu.VMEM((NSEG, SEG, HD), bf16),
            pltpu.VMEM((NSEG, SEG, HD), bf16),
            pltpu.VMEM((NSEG, HD, SEG), bf16),
            pltpu.VMEM((SEG, HD), bf16),
            pltpu.VMEM((SEG, HD), bf16),
            pltpu.VMEM((NSEG, SEG, SEG), f32),
            pltpu.VMEM((NSEG, SEG, SEG), f32),
            pltpu.VMEM((NSEG, SEG, SEG), f32),
            pltpu.VMEM((NSEG, SEG, HD), f32),
            pltpu.VMEM((NSEG, SEG, HD), f32),
            pltpu.VMEM((1, SEG), f32),
            pltpu.VMEM((1, SEG), f32),
            pltpu.VMEM((HD, SEG), f32),
            pltpu.VMEM((SEG, SEG), bf16),
        ],
        compiler_params=pltpu.CompilerParams(vmem_limit_bytes=58 << 20),
        cost_estimate=pl.CostEstimate(
            flops=20_000_000_000, bytes_accessed=8_000_000, transcendentals=16_000_000
        ),
        name="attention",
    )(sc, qd, kv0, kv1, kv2, kv3)


def pair_sum_kernel(a_ref, b_ref, out_ref):
    out_ref[...] = (a_ref[...].astype(f32) + b_ref[...].astype(f32)).astype(bf16)


def pair_sum(a, b):
    return pl.pallas_call(
        pair_sum_kernel,
        out_shape=jax.ShapeDtypeStruct(a.shape, bf16),
        in_specs=[VM, VM],
        out_specs=VM,
        name="pair_sum",
    )(a, b)


def last_sum_kernel(a_ref, b_ref, c_ref, out_ref):
    out_ref[...] = (a_ref[...] + b_ref[...].astype(f32) + c_ref[...].astype(f32)).astype(bf16)


def last_sum(a, b, c):
    return pl.pallas_call(
        last_sum_kernel,
        out_shape=jax.ShapeDtypeStruct(a.shape, bf16),
        in_specs=[VM] * 3,
        out_specs=VM,
        name="last_sum",
    )(a, b, c)


def unpack_kernel(dq_ref, dkv_ref, q_ref, k_ref, v_ref):
    for h in range(KVH):
        q_ref[:, h * 2 * HD : (h + 1) * 2 * HD] = dq_ref[h]
        k_ref[:, h * HD : (h + 1) * HD] = dkv_ref[h, :, :HD]
        v_ref[:, h * HD : (h + 1) * HD] = dkv_ref[h, :, HD:]


def unpack(dq, dkv):
    return pl.pallas_call(
        unpack_kernel,
        out_shape=(
            jax.ShapeDtypeStruct((TOK, 2 * KVH * HD), bf16),
            jax.ShapeDtypeStruct((TOK, KVH * HD), bf16),
            jax.ShapeDtypeStruct((TOK, KVH * HD), bf16),
        ),
        in_specs=[VM, VM],
        out_specs=(VM, VM, VM),
        name="unpack",
    )(dq, dkv)


def project_kernel(sc_ref, tok_ref, wk_ref, wv_ref, embed_ref, out_ref, xk_s, xv_s, sq, cross):
    step = pl.program_id(0)

    @pl.when(step == 0)
    def _():
        for h in range(KVH):
            base = (h // 2) * 8 + (h % 2) * 2
            total = tok_ref[base].astype(f32) + tok_ref[base + 1].astype(f32)
            total = total + tok_ref[base + 4].astype(f32) + tok_ref[base + 5].astype(f32)
            total = total.astype(bf16)
            xk_s[:, h * HD : (h + 1) * HD] = total[:, :HD]
            xv_s[:, h * HD : (h + 1) * HD] = total[:, HD:]
        sq[...] = jnp.zeros_like(sq)
        cross[...] = jnp.zeros_like(cross)

    projected = mm(xk_s[...], wk_ref[...], NT) + mm(xv_s[...], wv_ref[...], NT)
    token = lax.broadcasted_iota(jnp.int32, (SLOTS, FS), 0) * 32 + sc_ref[1]
    grad = jnp.where(token < sc_ref[0], projected, 0.0).astype(bf16)
    out_ref[step, :, :FS] = grad
    rows = embed_ref[0, :SLOTS, :].astype(f32)
    tail = embed_ref[0, SLOTS:, :].astype(f32)
    scale = tail[0:1] + tail[1:2] + tail[2:3]
    sq[...] += jnp.sum(rows * rows, 1, keepdims=True)
    cross[...] += jnp.sum(rows * (scale * grad.astype(f32)), 1, keepdims=True)

    @pl.when(step == NDP - 1)
    def _():
        lane = lax.broadcasted_iota(jnp.int32, (SLOTS, 128), 1)
        inv = lax.rsqrt(sq[...] / D + norm_eps)
        parts = split3(inv) + split3(cross[...] / D)
        tail = jnp.zeros((SLOTS, 128), f32)
        for n, part in enumerate(parts):
            tail = jnp.where(lane == n, part.astype(f32), tail)
        for n in range(NDP):
            out_ref[n, :, FS:] = tail.astype(bf16)


def project(sc, tok, wk, wv, embed):
    return pl.pallas_call(
        project_kernel,
        out_shape=jax.ShapeDtypeStruct((NDP, SLOTS, FS + 128), bf16),
        grid=(NDP,),
        in_specs=[
            SM,
            pl.BlockSpec((32, SLOTS, 2 * HD), lambda n: (0, 0, 0)),
            pl.BlockSpec((FS, KVH * HD), lambda n: (n, 0)),
            pl.BlockSpec((FS, KVH * HD), lambda n: (n, 0)),
            pl.BlockSpec((1, SLOTS + 16, FS), lambda n: (n, 0, 0)),
        ],
        out_specs=pl.BlockSpec((NDP, SLOTS, FS + 128), lambda n: (0, 0, 0)),
        scratch_shapes=[
            pltpu.VMEM((SLOTS, KVH * HD), bf16),
            pltpu.VMEM((SLOTS, KVH * HD), bf16),
            pltpu.VMEM((SLOTS, 1), f32),
            pltpu.VMEM((SLOTS, 1), f32),
        ],
        compiler_params=pltpu.CompilerParams(vmem_limit_bytes=32 << 20),
        cost_estimate=pl.CostEstimate(
            flops=1_200_000_000, bytes_accessed=21_000_000, transcendentals=0
        ),
        name="project",
    )(sc, tok, wk, wv, embed)


def norm_kernel(owner_ref, recv_ref, embed_ref, scale_ref, out_ref):
    tail = recv_ref[0, :, FS:].astype(f32)
    lane = lax.broadcasted_iota(jnp.int32, (SLOTS, 128), 1)
    inv = jnp.sum(jnp.where(lane < 3, tail, 0.0), 1, keepdims=True)
    cross = jnp.sum(jnp.where(lane >= 3, tail, 0.0), 1, keepdims=True)
    scaled = scale_ref[...] * recv_ref[0, :, :FS].astype(f32)
    rows = embed_ref[0].astype(f32)
    out_ref[0] = inv * scaled - rows * (inv * inv * inv * cross)


def norm_grads(owner, recv, embed, scale):
    return pl.pallas_call(
        norm_kernel,
        out_shape=jax.ShapeDtypeStruct((NDP, SLOTS, FS), f32),
        grid_spec=pltpu.PrefetchScalarGridSpec(
            num_scalar_prefetch=1,
            grid=(NDP,),
            in_specs=[
                pl.BlockSpec((1, SLOTS, FS + 128), lambda b, owner: (b, 0, 0)),
                pl.BlockSpec((1, SLOTS, FS), lambda b, owner: (owner[b], 0, 0)),
                pl.BlockSpec((1, FS), lambda b, owner: (0, 0)),
            ],
            out_specs=pl.BlockSpec((1, SLOTS, FS), lambda b, owner: (owner[b], 0, 0)),
        ),
        name="norm_grads",
    )(owner, recv, embed, scale)


def exchange(x, axes):
    return lax.all_to_all(x, axes, split_axis=0, concat_axis=0, tiled=True)


def swap(x, axis):
    return lax.ppermute(x, axis, [(0, 1), (1, 0)])


def local(
    query_states,
    key_states,
    value_states,
    out_grads,
    image_counts,
    prefix_lengths,
    encoder_owner,
    key_weight,
    value_weight,
    norm_scale,
    image_embed,
):
    ctx = ("y", "zh", "zl", "core")
    scale = norm_scale.reshape(1, FS)
    sc = jnp.stack([prefix_lengths[0], lax.axis_index("zh"), lax.axis_index("core")]).astype(
        jnp.int32
    )
    tok_sc = jnp.stack([image_counts[0], lax.axis_index(ctx)]).astype(jnp.int32)

    kv0 = exchange(pack_heads(key_states[0], value_states[0], "pack_kv"), ("y", "zl"))
    kv1 = swap(kv0, "core")
    kv2 = swap(kv0, "zh")
    kv3 = swap(kv2, "core")
    qd = exchange(pack_heads(query_states[0], out_grads[0], "pack_qd"), ("y", "zl"))
    embed_full = exchange(pack_embed(encoder_owner, image_embed, scale), "dp")

    dq, own, core_part, far, farcore, tok = attention(sc, qd, kv0, kv1, kv2, kv3)

    tok_in = exchange(tok, ctx)
    far_sum = pair_sum(far, swap(farcore, "core"))
    dkv = last_sum(own, swap(core_part, "core"), swap(far_sum, "zh"))
    payload = project(tok_sc, tok_in, key_weight, value_weight, embed_full)
    recv = exchange(payload, "dp")
    dq_in = exchange(dq, ("y", "zl"))
    dkv_in = exchange(dkv, ("y", "zl"))
    image_grads = norm_grads(encoder_owner, recv, image_embed, scale)
    query_grads, key_grads, value_grads = unpack(dq_in, dkv_in)
    return (query_grads[None], key_grads[None], value_grads[None], image_grads)


def solution(mesh):
    ctx = ("y", "zh", "zl", "core")
    split = Mesh(mesh.devices.reshape(4, 4, 2, 2, 2), ("dp",) + ctx)
    rows = P("dp", ctx, None)
    image = P(None, ctx, "dp")
    in_specs = (rows, rows, rows, rows, P("dp"), P("dp"), P(), P(), P(), P("dp"), image)
    out_specs = (rows, rows, rows, image)
    return jax.shard_map(local, mesh=split, in_specs=in_specs, out_specs=out_specs, check_vma=False)
```

time: 661 us -> 171 us (0.26)
  waiting for transfers between devices: 284 us -> 43.6 us
  matrix products: 146 us -> 0 us
  local copies, waits for them, and re-layouts: 133 us -> 12 us
  Pallas kernels: 0 us -> 62.5 us
  other arithmetic: 35.3 us -> 0.72 us
  starting transfers between devices: 5.68 us -> 32.5 us
  blocking collectives: 35 us -> 15.6 us
  between operations: 14.6 us -> 2.07 us
    reduce_scatter x2 -> x0, waiting for transfers between devices: 170 us -> none  [the longest x1 89.7 us: local(): lax.psum_scatter(value_part.astype(jnp.bfloat16), 'ctx', scatter_dimensio...]
    dot_general x59 -> x0, matrix products: 146 us -> none  [the longest x16 49 us: value_scores(): jnp.einsum('qgmd,kgd->gmqk', grad_four, value_heads, preferred_element_ty...]
    all_gather x2 -> x0, waiting for transfers between devices: 95.7 us -> none  [the longest x1 52.4 us: local(): lax.all_gather(key_states[0], 'ctx', axis=0, tiled=True)]
    pallas_call x0 -> x9, Pallas kernels: none -> 62.5 us  [the longest x1 35 us: attention(): pl.pallas_call(attention_kernel, out_shape=(jax.ShapeDtypeStruct(part, bf...]
    dynamic_slice x48 -> x0, local copies, waits for them, and re-layouts: 57.4 us -> none  [row_stats(): lax.scan(stats_step, (stat_zero, stat_zero), (key_steps, value_steps, sta...]
    convert_element_type x3 -> x0, local copies, waits for them, and re-layouts: 24 us -> none  [the longest x1 11.5 us: local(): key_part.astype(jnp.bfloat16)]
    all_to_all x1 -> x6, starting transfers between devices: 5.34 us -> 26.7 us  [exchange(): return lax.all_to_all(x, axes, split_axis=0, concat_axis=0, tiled=True)]
    lt x17 -> x0, other arithmetic: 20.7 us -> none  [the longest x16 20.7 us: visibility(): key_pos[None, :] < prefix]
  transfers between devices with their start and end apart: 5 -> 12, of which waited for: 5 -> 4; matrix products, arithmetic and copies ran while one was open for 5% -> 1% of each run, Pallas kernels for 0% -> 34%
where the time goes in v1:
time: 171 us; the launch traced here: 169 us
  Pallas kernels  62.5 us (37%)
  waiting for transfers between devices  43.6 us (25%)
  starting transfers between devices  32.5 us (19%)
  blocking collectives  15.6 us (9%)
  local copies, waits for them, and re-layouts  12 us (7%)
  between operations  2.07 us (1%)
    pallas_call x1, Pallas kernels, attention(): pl.pallas_call(attention_kernel, out_shape=(jax.ShapeDtypeStruct(part, bf...  35 us
    all_to_all x6, waiting for transfers between devices, exchange(): return lax.all_to_all(x, axes, split_axis=0, concat_axis=0, tiled=True)  29.1 us
    all_to_all x6, starting transfers between devices, exchange(): return lax.all_to_all(x, axes, split_axis=0, concat_axis=0, tiled=True)  26.7 us
    all_to_all x1, blocking collectives, exchange(): return lax.all_to_all(x, axes, split_axis=0, concat_axis=0, tiled=True)  15.6 us
    ppermute x6, waiting for transfers between devices, swap(): return lax.ppermute(x, axis, [(0, 1), (1, 0)])  14.5 us
    unnamed x24, local copies, waits for them, and re-layouts  10.7 us
    pallas_call x1, Pallas kernels, project(): pl.pallas_call(project_kernel, out_shape=jax.ShapeDtypeStruct((NDP, SLOTS...  8.21 us
    ppermute x6, starting transfers between devices, swap(): return lax.ppermute(x, axis, [(0, 1), (1, 0)])  5.86 us
  transfers between devices with their start and end apart: 12, of which 4 were waited for; matrix products, arithmetic and copies ran while one was open for 1% of the time, Pallas kernels for 34%

profile of v1, /device:TPU:0, one launch (start us, length us, event | category | flops | bytes accessed | tf_op | source)
XLA Modules:
  0.0 169.1 jit_solution(15169212883273408265)
XLA Ops:
  0.6 1.9 %pack_kv.1 = bf16[8,128,256]{2,1,0:T(8,128)(2,1)} custom-call(bf16[128,1024]{1,0:T(8,128)(2,1)} %bitcast.12, bf16[128,1024]{1,0:T(8,128)(2,1)} %bitcast.13), custom_call_target="tpu_custom_call" | custom-call | tf_op jit(solution)/shard_map/pack_kv/pallas_call | solution.py:55
  2.5 15.6 %all_to_all.35.kv0_ref = bf16[8,128,256]{2,1,0:T(8,128)(2,1)S(1)} all-to-all(bf16[8,128,256]{2,1,0:T(8,128)(2,1)} %pack_kv.1), channel_id=1, replica_groups=mesh['dp'=4,'y'=4,'zh'=2,'zl'=2,'core'=2] {'y','zl'}, dimensions={0} | all-to-all | bytes 1048576 | tf_op jit(solution)/shard_map/all_to_all | solution.py:410
  18.2 3.6 %collective-permute-start.1 = (bf16[8,128,256]{2,1,0:T(8,128)(2,1)S(1)}, bf16[8,128,256]{2,1,0:T(8,128)(2,1)S(1)}, u32[]{:S(2)}, u32[]{:S(2)}) collective-permute-start(bf16[8,128,256]{2,1,0:T(8,128)(2,1)S(1)} %all_to_all.35.kv0_ref), channel_id=1, source_target_pairs={{0,4},{4,0},{1,5},{5,1},{2,6},{6,2},{3,7},{7,3},{8,12},{12,8},{9,1... | collective-permute-start | bytes 1572872 | tf_op jit(solution)/shard_map/ppermute | solution.py:414
  21.8 2.3 %pack_qd.1 = bf16[8,128,512]{2,1,0:T(8,128)(2,1)} custom-call(bf16[128,2048]{1,0:T(8,128)(2,1)} %bitcast.10, bf16[128,2048]{1,0:T(8,128)(2,1)} %bitcast.11), custom_call_target="tpu_custom_call" | custom-call | tf_op jit(solution)/shard_map/pack_qd/pallas_call | solution.py:55
  24.0 3.6 %all-to-all-start = ((bf16[8,128,512]{2,1,0:T(8,128)(2,1)}), bf16[8,128,512]{2,1,0:T(8,128)(2,1)S(1)}, u32[]{:S(2)}, u32[]{:S(2)}) async-start(bf16[8,128,512]{2,1,0:T(8,128)(2,1)} %pack_qd.1), calls=%async_computation | async-start | bytes 2097152 | tf_op jit(solution)/shard_map/all_to_all | solution.py:410
  27.7 14.4 %collective-permute-done.1.kv2_ref = bf16[8,128,256]{2,1,0:T(8,128)(2,1)S(1)} collective-permute-done((bf16[8,128,256]{2,1,0:T(8,128)(2,1)S(1)}, bf16[8,128,256]{2,1,0:T(8,128)(2,1)S(1)}, u32[]{:S(2)}, u32[]{:S(2)}) %collective-permute-start.1) | collective-permute-done | bytes 524320 | tf_op jit(solution)/shard_map/ppermute | solution.py:414
  44.1 4.0 %pack_embed.1 = bf16[4,80,1152]{2,1,0:T(8,128)(2,1)} custom-call(s32[4]{0:T(128)} %owner_ref.3, bf16[4,64,1152]{2,1,0:T(8,128)(2,1)} %embed_ref.3, f32[1,1152]{1,0:T(1,128)} %reshape.11.scale_ref), custom_call_target="tpu_custom_call" | custom-call | tf_op jit(solution)/shard_map/pack_embed/pallas_call | solution.py:74
  48.7 4.3 %all-to-all-start.5 = ((bf16[4,80,1152]{2,1,0:T(8,128)(2,1)}), bf16[4,80,1152]{2,1,0:T(8,128)(2,1)S(1)}, u32[]{:S(2)}, u32[]{:S(2)}) async-start(bf16[4,80,1152]{2,1,0:T(8,128)(2,1)} %pack_embed.1), calls=%async_computation.5 | async-start | bytes 1474560 | tf_op jit(solution)/shard_map/all_to_all | solution.py:410
  53.8 35.0 %attention.1 = (bf16[8,128,256]{2,1,0:T(8,128)(2,1)}, f32[8,128,256]{2,1,0:T(8,128)}, bf16[8,128,256]{2,1,0:T(8,128)(2,1)}, bf16[8,128,256]{2,1,0:T(8,128)(2,1)}...) custom-call(s32[3]{0:T(128)} %pad_add_fusion.sc_ref, bf16[8,128,512]{2,1,0:T(8,128)(2,1)} %copy-done.5, ...), custom_call_target="tpu_custom_call" | custom-call | flops 20000000000 | bytes 8000000 | tf_op jit(solution)/shard_map/attention/pallas_call | solution.py:232
  88.7 6.8 %all-to-all-start.4 = ((bf16[32,64,256]{2,1,0:T(8,128)(2,1)}), bf16[32,64,256]{2,1,0:T(8,128)(2,1)S(1)}, u32[]{:S(2)}, u32[]{:S(2)}) async-start(bf16[32,64,256]{2,1,0:T(8,128)(2,1)} %get-tuple-element.21), calls=%async_computation.4 | async-start | bytes 2097152 | tf_op jit(solution)/shard_map/all_to_all | solution.py:410
  95.9 16.5 %all-to-all-done.4.tok_ref = bf16[32,64,256]{2,1,0:T(8,128)(2,1)S(1)} async-done(((bf16[32,64,256]{2,1,0:T(8,128)(2,1)}), bf16[32,64,256]{2,1,0:T(8,128)(2,1)S(1)}, u32[]{:S(2)}, u32[]{:S(2)}) %all-to-all-start.4) | async-done | bytes 1048608 | tf_op jit(solution)/shard_map/all_to_all | solution.py:410
  112.4 3.5 %all-to-all-start.2 = ((bf16[8,128,256]{2,1,0:T(8,128)(2,1)}), bf16[8,128,256]{2,1,0:T(8,128)(2,1)S(1)}, u32[]{:S(2)}, u32[]{:S(2)}) async-start(bf16[8,128,256]{2,1,0:T(8,128)(2,1)} %get-tuple-element.13), calls=%async_computation.2 | async-start | bytes 1048576 | tf_op jit(solution)/shard_map/all_to_all | solution.py:410
  117.8 2.1 %pair_sum.1 = bf16[8,128,256]{2,1,0:T(8,128)(2,1)} custom-call(bf16[8,128,256]{2,1,0:T(8,128)(2,1)} %get-tuple-element.16.a_ref, bf16[8,128,256]{2,1,0:T(8,128)(2,1)} %copy-done.6), custom_call_target="tpu_custom_call" | custom-call | tf_op jit(solution)/shard_map/pair_sum/pallas_call | solution.py:273
  119.9 1.4 collective-permute-start.5
  121.4 3.7 %copy-done = bf16[4608,1024]{1,0:T(8,128)(2,1)S(1)} copy-done((bf16[4608,1024]{1,0:T(8,128)(2,1)S(1)}, bf16[4608,1024]{1,0:T(8,128)(2,1)}, u32[]{:S(2)}) %copy-start) | copy-done | bytes 9437208
  125.1 3.7 %copy-done.1 = bf16[4608,1024]{1,0:T(8,128)(2,1)S(1)} copy-done((bf16[4608,1024]{1,0:T(8,128)(2,1)S(1)}, bf16[4608,1024]{1,0:T(8,128)(2,1)}, u32[]{:S(2)}) %copy-start.1) | copy-done | bytes 9437208
  128.7 8.2 %project.1 = bf16[4,64,1280]{2,1,0:T(8,128)(2,1)} custom-call(s32[2]{0:T(128)S(1)} %pad_add_fusion.1.sc_ref, bf16[32,64,256]{2,1,0:T(8,128)(2,1)S(1)} %all-to-all-done.4.tok_ref, bf16[4608,1024]{1,0:T(8,128)(2,1)S(1)} %copy-done, bf16[4608,1024]{1,0:T(8,128)(2,1)S(1)} %copy-done.1, bf16[4,80,1152]{2,1,0:T(8,128)(2,1)S(1)} %all-to-all-done.5.embed_ref), custom_call_target="tpu_custom_call" | custom-call | flops 1200000000 | bytes 21000000 | tf_op jit(solution)/shard_map/project/pallas_call | solution.py:355
  137.0 3.5 %all-to-all-start.6 = ((bf16[4,64,1280]{2,1,0:T(8,128)(2,1)}), bf16[4,64,1280]{2,1,0:T(8,128)(2,1)S(1)}, u32[]{:S(2)}, u32[]{:S(2)}) async-start(bf16[4,64,1280]{2,1,0:T(8,128)(2,1)} %project.1), calls=%async_computation.6 | async-start | bytes 1310720 | tf_op jit(solution)/shard_map/all_to_all | solution.py:410
  141.4 2.5 %last_sum.1 = bf16[8,128,256]{2,1,0:T(8,128)(2,1)} custom-call(f32[8,128,256]{2,1,0:T(8,128)} %get-tuple-element.14.a_ref, bf16[8,128,256]{2,1,0:T(8,128)(2,1)} %copy-done.7, bf16[8,128,256]{2,1,0:T(8,128)(2,1)} %copy-done.8), custom_call_target="tpu_custom_call" | custom-call | tf_op jit(solution)/shard_map/last_sum/pallas_call | solution.py:287
  143.9 8.0 %all-to-all-done.6.recv_ref = bf16[4,64,1280]{2,1,0:T(8,128)(2,1)S(1)} async-done(((bf16[4,64,1280]{2,1,0:T(8,128)(2,1)}), bf16[4,64,1280]{2,1,0:T(8,128)(2,1)S(1)}, u32[]{:S(2)}, u32[]{:S(2)}) %all-to-all-start.6) | async-done | bytes 655392 | tf_op jit(solution)/shard_map/all_to_all | solution.py:410
  151.9 5.0 %all-to-all-start.3 = ((bf16[8,128,256]{2,1,0:T(8,128)(2,1)}), bf16[8,128,256]{2,1,0:T(8,128)(2,1)S(1)}, u32[]{:S(2)}, u32[]{:S(2)}) async-start(bf16[8,128,256]{2,1,0:T(8,128)(2,1)} %last_sum.1), calls=%async_computation.3 | async-start | bytes 1048576 | tf_op jit(solution)/shard_map/all_to_all | solution.py:410
  157.0 4.4 %norm_grads.1 = f32[4,64,1152]{2,1,0:T(8,128)} custom-call(s32[4]{0:T(128)} %owner_ref.3, bf16[4,64,1280]{2,1,0:T(8,128)(2,1)} %copy-done.2, bf16[4,64,1152]{2,1,0:T(8,128)(2,1)} %embed_ref.3, f32[1,1152]{1,0:T(1,128)} %reshape.11.scale_ref), custom_call_target="tpu_custom_call" | custom-call | tf_op jit(solution)/shard_map/norm_grads/pallas_call | solution.py:392
  161.3 4.6 %all-to-all-done.3.dkv_ref = bf16[8,128,256]{2,1,0:T(8,128)(2,1)S(1)} async-done(((bf16[8,128,256]{2,1,0:T(8,128)(2,1)}), bf16[8,128,256]{2,1,0:T(8,128)(2,1)S(1)}, u32[]{:S(2)}, u32[]{:S(2)}) %all-to-all-start.3) | async-done | bytes 524320 | tf_op jit(solution)/shard_map/all_to_all | solution.py:410
  166.8 2.3 %unpack.1 = (bf16[128,2048]{1,0:T(8,128)(2,1)}, bf16[128,1024]{1,0:T(8,128)(2,1)}, bf16[128,1024]{1,0:T(8,128)(2,1)}) custom-call(bf16[8,128,256]{2,1,0:T(8,128)(2,1)} %copy-done.3, bf16[8,128,256]{2,1,0:T(8,128)(2,1)} %copy-done.4), custom_call_target="tpu_custom_call" | custom-call | tf_op jit(solution)/shard_map/unpack/pallas_call | solution.py:304
  (37 shorter events, 6.2 us)
Async XLA Ops:
  18.2 34.8 %copy-start.9 = (bf16[8,128,256]{2,1,0:T(8,128)(2,1)}, bf16[8,128,256]{2,1,0:T(8,128)(2,1)S(1)}, u32[]{:S(2)}) copy-start(bf16[8,128,256]{2,1,0:T(8,128)(2,1)S(1)} %all_to_all.35.kv0_ref) | copy-start | bytes 1572868
  18.2 23.9 %collective-permute-start.1 = (bf16[8,128,256]{2,1,0:T(8,128)(2,1)S(1)}, bf16[8,128,256]{2,1,0:T(8,128)(2,1)S(1)}, u32[]{:S(2)}, u32[]{:S(2)}) collective-permute-start(bf16[8,128,256]{2,1,0:T(8,128)(2,1)S(1)} %all_to_all.35.kv0_ref), channel_id=1, source_target_pairs={{0,4},{4,0},{1,5},{5,1},{2,6},{6,2},{3,7},{7,3},{8,12},{12,8},{9,1... | collective-permute-start | bytes 1572872 | tf_op jit(solution)/shard_map/ppermute | solution.py:414
  24.0 24.7 %all-to-all-start = ((bf16[8,128,512]{2,1,0:T(8,128)(2,1)}), bf16[8,128,512]{2,1,0:T(8,128)(2,1)S(1)}, u32[]{:S(2)}, u32[]{:S(2)}) async-start(bf16[8,128,512]{2,1,0:T(8,128)(2,1)} %pack_qd.1), calls=%async_computation | async-start | bytes 2097152 | tf_op jit(solution)/shard_map/all_to_all | solution.py:410
  27.6 25.4 %collective-permute-start = (bf16[8,128,256]{2,1,0:T(8,128)(2,1)S(1)}, bf16[8,128,256]{2,1,0:T(8,128)(2,1)S(1)}, u32[]{:S(2)}, u32[]{:S(2)}) collective-permute-start(bf16[8,128,256]{2,1,0:T(8,128)(2,1)S(1)} %all_to_all.35.kv0_ref), channel_id=1, source_target_pairs={{0,1},{1,0},{2,3},{3,2},{4,5},{5,4},{6,7},{7,6},{8,9},{9,8},{10,11... | collective-permute-start | bytes 1572872 | tf_op jit(solution)/shard_map/ppermute | solution.py:414
  42.1 10.9 %copy-start.10 = (bf16[8,128,256]{2,1,0:T(8,128)(2,1)}, bf16[8,128,256]{2,1,0:T(8,128)(2,1)S(1)}, u32[]{:S(2)}) copy-start(bf16[8,128,256]{2,1,0:T(8,128)(2,1)S(1)} %collective-permute-done.1.kv2_ref) | copy-start | bytes 1572868
  42.1 10.9 %collective-permute-start.2 = (bf16[8,128,256]{2,1,0:T(8,128)(2,1)S(1)}, bf16[8,128,256]{2,1,0:T(8,128)(2,1)}, u32[]{:S(2)}, u32[]{:S(2)}) collective-permute-start(bf16[8,128,256]{2,1,0:T(8,128)(2,1)S(1)} %collective-permute-done.1.kv2_ref), channel_id=1, source_target_pairs={{0,1},{1,0},{2,3},{3,2},{4,5},{5,4},{6,7},{7,6},{8,9},{9,8},{10,11... | collective-permute-start | bytes 1572872 | tf_op jit(solution)/shard_map/ppermute | solution.py:414
  48.7 4.3 %copy-start.5 = (bf16[8,128,512]{2,1,0:T(8,128)(2,1)}, bf16[8,128,512]{2,1,0:T(8,128)(2,1)S(1)}, u32[]{:S(2)}) copy-start(bf16[8,128,512]{2,1,0:T(8,128)(2,1)S(1)} %all-to-all-done.qd_ref) | copy-start | bytes 3145732
  48.7 40.1 %all-to-all-start.5 = ((bf16[4,80,1152]{2,1,0:T(8,128)(2,1)}), bf16[4,80,1152]{2,1,0:T(8,128)(2,1)S(1)}, u32[]{:S(2)}, u32[]{:S(2)}) async-start(bf16[4,80,1152]{2,1,0:T(8,128)(2,1)} %pack_embed.1), calls=%async_computation.5 | async-start | bytes 1474560 | tf_op jit(solution)/shard_map/all_to_all | solution.py:410
  53.0 0.8 copy-start.11
  88.7 23.6 %all-to-all-start.4 = ((bf16[32,64,256]{2,1,0:T(8,128)(2,1)}), bf16[32,64,256]{2,1,0:T(8,128)(2,1)S(1)}, u32[]{:S(2)}, u32[]{:S(2)}) async-start(bf16[32,64,256]{2,1,0:T(8,128)(2,1)} %get-tuple-element.21), calls=%async_computation.4 | async-start | bytes 2097152 | tf_op jit(solution)/shard_map/all_to_all | solution.py:410
  95.6 21.4 %collective-permute-start.4 = (bf16[8,128,256]{2,1,0:T(8,128)(2,1)}, bf16[8,128,256]{2,1,0:T(8,128)(2,1)S(1)}, u32[]{:S(2)}, u32[]{:S(2)}) collective-permute-start(bf16[8,128,256]{2,1,0:T(8,128)(2,1)} %get-tuple-element.17), channel_id=1, source_target_pairs={{0,1},{1,0},{2,3},{3,2},{4,5},{5,4},{6,7},{7,6},{8,9},{9,8},{10,11... | collective-permute-start | bytes 1572872 | tf_op jit(solution)/shard_map/ppermute | solution.py:414
  112.4 24.6 %all-to-all-start.2 = ((bf16[8,128,256]{2,1,0:T(8,128)(2,1)}), bf16[8,128,256]{2,1,0:T(8,128)(2,1)S(1)}, u32[]{:S(2)}, u32[]{:S(2)}) async-start(bf16[8,128,256]{2,1,0:T(8,128)(2,1)} %get-tuple-element.13), calls=%async_computation.2 | async-start | bytes 1048576 | tf_op jit(solution)/shard_map/all_to_all | solution.py:410
  116.6 23.8 %collective-permute-start.3 = (bf16[8,128,256]{2,1,0:T(8,128)(2,1)}, bf16[8,128,256]{2,1,0:T(8,128)(2,1)S(1)}, u32[]{:S(2)}, u32[]{:S(2)}) collective-permute-start(bf16[8,128,256]{2,1,0:T(8,128)(2,1)} %get-tuple-element.15), channel_id=1, source_target_pairs={{0,1},{1,0},{2,3},{3,2},{4,5},{5,4},{6,7},{7,6},{8,9},{9,8},{10,11... | collective-permute-start | bytes 1572872 | tf_op jit(solution)/shard_map/ppermute | solution.py:414
  117.0 0.8 copy-start.6
  119.9 20.5 %collective-permute-start.5 = (bf16[8,128,256]{2,1,0:T(8,128)(2,1)}, bf16[8,128,256]{2,1,0:T(8,128)(2,1)S(1)}, u32[]{:S(2)}, u32[]{:S(2)}) collective-permute-start(bf16[8,128,256]{2,1,0:T(8,128)(2,1)} %pair_sum.1), channel_id=1, source_target_pairs={{0,4},{4,0},{1,5},{5,1},{2,6},{6,2},{3,7},{7,3},{8,12},{12,8},{9,1... | collective-permute-start | bytes 1572872 | tf_op jit(solution)/shard_map/ppermute | solution.py:414
  121.4 3.7 %copy-start = (bf16[4608,1024]{1,0:T(8,128)(2,1)S(1)}, bf16[4608,1024]{1,0:T(8,128)(2,1)}, u32[]{:S(2)}) copy-start(bf16[4608,1024]{1,0:T(8,128)(2,1)} %wk_ref.1) | copy-start | bytes 28311556
  125.1 3.7 %copy-start.1 = (bf16[4608,1024]{1,0:T(8,128)(2,1)S(1)}, bf16[4608,1024]{1,0:T(8,128)(2,1)}, u32[]{:S(2)}) copy-start(bf16[4608,1024]{1,0:T(8,128)(2,1)} %wv_ref.1) | copy-start | bytes 28311556
  137.0 29.0 %copy-start.3 = (bf16[8,128,256]{2,1,0:T(8,128)(2,1)}, bf16[8,128,256]{2,1,0:T(8,128)(2,1)S(1)}, u32[]{:S(2)}) copy-start(bf16[8,128,256]{2,1,0:T(8,128)(2,1)S(1)} %all-to-all-done.2.dq_ref) | copy-start | bytes 1572868
  137.0 15.0 %all-to-all-start.6 = ((bf16[4,64,1280]{2,1,0:T(8,128)(2,1)}), bf16[4,64,1280]{2,1,0:T(8,128)(2,1)S(1)}, u32[]{:S(2)}, u32[]{:S(2)}) async-start(bf16[4,64,1280]{2,1,0:T(8,128)(2,1)} %project.1), calls=%async_computation.6 | async-start | bytes 1310720 | tf_op jit(solution)/shard_map/all_to_all | solution.py:410
  140.5 0.8 copy-start.7
  140.5 1.0 copy-start.8
  151.9 5.0 %copy-start.2 = (bf16[4,64,1280]{2,1,0:T(8,128)(2,1)}, bf16[4,64,1280]{2,1,0:T(8,128)(2,1)S(1)}, u32[]{:S(2)}) copy-start(bf16[4,64,1280]{2,1,0:T(8,128)(2,1)S(1)} %all-to-all-done.6.recv_ref) | copy-start | bytes 1966084
  151.9 14.0 %all-to-all-start.3 = ((bf16[8,128,256]{2,1,0:T(8,128)(2,1)}), bf16[8,128,256]{2,1,0:T(8,128)(2,1)S(1)}, u32[]{:S(2)}, u32[]{:S(2)}) async-start(bf16[8,128,256]{2,1,0:T(8,128)(2,1)} %last_sum.1), calls=%async_computation.3 | async-start | bytes 1048576 | tf_op jit(solution)/shard_map/all_to_all | solution.py:410
  166.0 0.8 copy-start.4

commit v2 on v1

v2 whole, which is shorter than its diff:
```python
import functools
import math

import jax
import jax.numpy as jnp
from jax import lax
from jax.experimental import pallas as pl
from jax.experimental.pallas import tpu as pltpu
from jax.sharding import Mesh, PartitionSpec as P

D = 4608
HD = 128
KVH = 8
TOK = 128
SLOTS = 64
NDP = 4
FS = D // NDP
SEG = 512
NSEG = 8

score_scale = 144.0 ** (-0.5)
soft_cap = 50.0
norm_eps = 1e-06
tanh_scale = score_scale / soft_cap
exp2_scale = soft_cap * math.log2(math.e)

f32 = jnp.float32
bf16 = jnp.bfloat16
VM = pl.BlockSpec(memory_space=pltpu.VMEM)
ANY = pl.BlockSpec(memory_space=pl.ANY)
SM = pl.BlockSpec(memory_space=pltpu.SMEM)
NT = (((1,), (1,)), ((), ()))
NN = (((1,), (0,)), ((), ()))


def mm(a, b, dims=NN):
    return lax.dot_general(a, b, dims, preferred_element_type=f32)


def split3(x):
    hi = x.astype(bf16)
    rest = x - hi.astype(f32)
    mid = rest.astype(bf16)
    lo = (rest - mid.astype(f32)).astype(bf16)
    return hi, mid, lo


def params(mib):
    return pltpu.CompilerParams(vmem_limit_bytes=mib << 20)


def cost(us, flops=0):
    return pl.CostEstimate(flops=flops, bytes_accessed=int(us * 3_000_000), transcendentals=0)


def pack_kernel(width, a_ref, b_ref, out_ref):
    for h in range(KVH):
        out_ref[h, :, :width] = a_ref[:, h * width : (h + 1) * width]
        out_ref[h, :, width:] = b_ref[:, h * width : (h + 1) * width]


def pack_heads(a, b, name):
    width = a.shape[1] // KVH
    return pl.pallas_call(
        functools.partial(pack_kernel, width),
        out_shape=jax.ShapeDtypeStruct((KVH, TOK, 2 * width), bf16),
        in_specs=[VM, VM],
        out_specs=VM,
        compiler_params=params(60),
        cost_estimate=cost(2),
        name=name,
    )(a, b)


def embed_pack_kernel(sc_ref, embed_ref, scale_ref, *out_refs):
    row = lax.broadcasted_iota(jnp.int32, (16, FS), 0)
    hi, mid, lo = split3(scale_ref[...].reshape(1, FS))
    parts = jnp.where(row == 0, hi.astype(f32), jnp.where(row == 1, mid.astype(f32), 0.0))
    parts = jnp.where(row == 2, lo.astype(f32), parts).astype(bf16)
    for n in range(NDP):
        out_refs[n][:SLOTS, :] = embed_ref[sc_ref[n]]
        out_refs[n][SLOTS:, :] = parts


def pack_embed(sc, embed, scale):
    one = jax.ShapeDtypeStruct((SLOTS + 16, FS), bf16)
    return pl.pallas_call(
        embed_pack_kernel,
        out_shape=(one,) * NDP,
        in_specs=[SM, VM, VM],
        out_specs=(VM,) * NDP,
        compiler_params=params(8),
        cost_estimate=cost(3),
        name="pack_embed",
    )(sc, embed, scale)


def attention_kernel(
    sc_ref,
    qd_ref,
    kv0_ref,
    kv1_ref,
    kv2_ref,
    kv3_ref,
    dq_ref,
    own_ref,
    core_ref,
    far_ref,
    farcore_ref,
    tok_ref,
    k_s,
    v_s,
    kt_s,
    q_s,
    do_s,
    e_s,
    w_s,
    p_s,
    dk_s,
    dv_s,
    tot,
    mom,
    dqt,
    perm,
    dot_s,
):
    prefix, zh, core = sc_ref[0], sc_ref[1], sc_ref[2]
    eye = (
        lax.broadcasted_iota(jnp.int32, (HD, HD), 0) == lax.broadcasted_iota(jnp.int32, (HD, HD), 1)
    ).astype(bf16)
    for seg in range(NSEG):
        near, away = ((kv0_ref, kv1_ref), (kv2_ref, kv3_ref))[seg // 4]
        y = seg % 4
        whole = jnp.concatenate([near[2 * y], near[2 * y + 1], away[2 * y], away[2 * y + 1]], 0)
        k_s[seg] = whole[:, :HD]
        v_s[seg] = whole[:, HD:]
        kt_s[seg] = mm(eye, whole[:, :HD], NT).astype(bf16)
    dk_s[...] = jnp.zeros_like(dk_s)
    dv_s[...] = jnp.zeros_like(dv_s)

    def key_start(j):
        far = j // 4
        return (j % 4) * 1024 + (zh + far - 2 * zh * far) * SEG

    def hidden(key0, row0):
        s = lax.broadcasted_iota(jnp.int32, (SEG, SEG), 0)
        piece = s // TOK
        other = piece // 2
        key = key0 + (piece % 2) * 256 + (core + other - 2 * core * other) * TOK + s % TOK
        lane = lax.broadcasted_iota(jnp.int32, (1, SEG), 1)
        row = row0 + ((lane // TOK) % 2) * 256 + lane % TOK
        return key >= jnp.maximum(row + 1, prefix)

    def row_body(i, _):
        row0 = i * 1024 + zh * SEG + core * TOK
        limit = jnp.maximum(prefix, row0 + 384)
        full = jnp.maximum(prefix, row0 + 1)
        for head in range(2):
            for z in range(2):
                at = pl.ds((head * 2 + z) * TOK, TOK)
                q_s[at, :] = qd_ref[2 * i + z, :, head * HD : (head + 1) * HD]
                do_s[at, :] = qd_ref[2 * i + z, :, (2 + head) * HD : (3 + head) * HD]
        tot[...] = jnp.zeros_like(tot)
        mom[...] = jnp.zeros_like(mom)
        dqt[...] = jnp.zeros_like(dqt)

        def scores(y, masked):
            pair = (y, y + 4)
            ts = [jnp.tanh(mm(k_s[j], q_s[...], NT) * tanh_scale) for j in pair]
            dps = [mm(v_s[j], do_s[...], NT) for j in pair]
            total, moment = tot[...], mom[...]
            for j, t, dp in zip(pair, ts, dps):
                e = jnp.exp2(t * exp2_scale)
                if masked:
                    e = jnp.where(hidden(key_start(j), row0), 0.0, e)
                total += jnp.sum(e, 0, keepdims=True)
                moment += jnp.sum(e * dp, 0, keepdims=True)
                e_s[j] = e.astype(bf16)
                w_s[j] = e * (1.0 - t * t)
                p_s[j] = dp
            tot[...], mom[...] = total, moment

        def first(y, _):
            @pl.when(y * 1024 + 1024 <= full)
            def _():
                scores(y, False)

            @pl.when((y * 1024 + 1024 > full) & (y * 1024 < limit))
            def _():
                scores(y, True)

            return 0

        lax.fori_loop(0, 4, first, 0)
        inv = 1.0 / tot[...]
        delta = mom[...] * inv
        dot_s[...] = (mm(eye, do_s[...], NT) * inv).astype(bf16)

        def second(y, _):
            @pl.when(y * 1024 < limit)
            def _():
                grad = dqt[...]
                for j in (y, y + 4):
                    ds = (w_s[j] * inv * (p_s[j] - delta)).astype(bf16)
                    dv_s[j] += mm(e_s[j], dot_s[...], NT)
                    dk_s[j] += mm(ds, q_s[...])
                    grad += mm(kt_s[j], ds)
                dqt[...] = grad

            return 0

        lax.fori_loop(0, 4, second, 0)
        dq = (dqt[...] * score_scale).T.astype(bf16)
        for head in range(2):
            for z in range(2):
                at = (head * 2 + z) * TOK
                dq_ref[2 * i + z, :, head * HD : (head + 1) * HD] = dq[at : at + TOK]
        return 0

    lax.fori_loop(0, 4, row_body, 0)

    out = lax.broadcasted_iota(jnp.int32, (SEG, SEG), 0)
    src = lax.broadcasted_iota(jnp.int32, (SEG, SEG), 1)
    slot = out % 16
    c_of = (slot // 4) % 2
    want = (
        (c_of + core - 2 * c_of * core) * 256 + (slot // 8) * TOK + (slot % 4) * 32 + out // 16
    )
    perm[...] = (want == src).astype(bf16)
    for seg in range(NSEG):
        near, away = ((own_ref, core_ref), (far_ref, farcore_ref))[seg // 4]
        y = seg % 4
        terms = jnp.concatenate([dk_s[seg] * score_scale, dv_s[seg]], 1)
        near[2 * y] = terms[:TOK].astype(near.dtype)
        near[2 * y + 1] = terms[TOK : 2 * TOK].astype(near.dtype)
        away[2 * y] = terms[2 * TOK : 3 * TOK].astype(away.dtype)
        away[2 * y + 1] = terms[3 * TOK :].astype(away.dtype)
        if y < 2:
            moved = mm(perm[...], terms.astype(bf16)).astype(bf16).reshape(32, 16, 2 * HD)
            z_at = zh if seg < 4 else 1 - zh
            tok_ref[:, pl.ds(pl.multiple_of((2 * y + z_at) * 16, 16), 16), :] = moved


def attention(sc, qd, kv0, kv1, kv2, kv3):
    part = (KVH, TOK, 2 * HD)
    return pl.pallas_call(
        attention_kernel,
        out_shape=(
            jax.ShapeDtypeStruct(part, bf16),
            jax.ShapeDtypeStruct(part, f32),
            jax.ShapeDtypeStruct(part, bf16),
            jax.ShapeDtypeStruct(part, bf16),
            jax.ShapeDtypeStruct(part, bf16),
            jax.ShapeDtypeStruct((32, SLOTS, 2 * HD), bf16),
        ),
        in_specs=[SM] + [VM] * 5,
        out_specs=(VM,) * 6,
        scratch_shapes=[
            pltpu.VMEM((NSEG, SEG, HD), bf16),
            pltpu.VMEM((NSEG, SEG, HD), bf16),
            pltpu.VMEM((NSEG, HD, SEG), bf16),
            pltpu.VMEM((SEG, HD), bf16),
            pltpu.VMEM((SEG, HD), bf16),
            pltpu.VMEM((NSEG, SEG, SEG), bf16),
            pltpu.VMEM((NSEG, SEG, SEG), f32),
            pltpu.VMEM((NSEG, SEG, SEG), f32),
            pltpu.VMEM((NSEG, SEG, HD), f32),
            pltpu.VMEM((NSEG, SEG, HD), f32),
            pltpu.VMEM((1, SEG), f32),
            pltpu.VMEM((1, SEG), f32),
            pltpu.VMEM((HD, SEG), f32),
            pltpu.VMEM((SEG, SEG), bf16),
            pltpu.VMEM((HD, SEG), bf16),
        ],
        compiler_params=params(60),
        cost_estimate=cost(36),
        name="attention",
    )(sc, qd, kv0, kv1, kv2, kv3)


def pair_sum_kernel(a_ref, b_ref, out_ref):
    out_ref[...] = (a_ref[...].astype(f32) + b_ref[...].astype(f32)).astype(bf16)


def pair_sum(a, b):
    return pl.pallas_call(
        pair_sum_kernel,
        out_shape=jax.ShapeDtypeStruct(a.shape, bf16),
        in_specs=[VM, VM],
        out_specs=VM,
        compiler_params=params(8),
        cost_estimate=cost(2),
        name="pair_sum",
    )(a, b)


def last_sum_kernel(dq_ref, a_ref, b_ref, c_ref, _, out_ref):
    out_ref[:, :, : 2 * HD] = dq_ref[...]
    total = a_ref[...] + b_ref[...].astype(f32) + c_ref[...].astype(f32)
    out_ref[:, :, 2 * HD :] = total.astype(bf16)


def last_sum(dq, a, b, c, after):
    return pl.pallas_call(
        last_sum_kernel,
        out_shape=jax.ShapeDtypeStruct((KVH, TOK, 4 * HD), bf16),
        in_specs=[VM] * 4 + [ANY],
        out_specs=VM,
        compiler_params=params(8),
        cost_estimate=cost(3),
        name="last_sum",
    )(dq, a, b, c, after)


def unpack_kernel(in_ref, q_ref, k_ref, v_ref):
    for h in range(KVH):
        q_ref[:, h * 2 * HD : (h + 1) * 2 * HD] = in_ref[h, :, : 2 * HD]
        k_ref[:, h * HD : (h + 1) * HD] = in_ref[h, :, 2 * HD : 3 * HD]
        v_ref[:, h * HD : (h + 1) * HD] = in_ref[h, :, 3 * HD :]


def unpack(grads):
    return pl.pallas_call(
        unpack_kernel,
        out_shape=(
            jax.ShapeDtypeStruct((TOK, 2 * KVH * HD), bf16),
            jax.ShapeDtypeStruct((TOK, KVH * HD), bf16),
            jax.ShapeDtypeStruct((TOK, KVH * HD), bf16),
        ),
        in_specs=[VM],
        out_specs=(VM, VM, VM),
        compiler_params=params(8),
        cost_estimate=cost(2),
        name="unpack",
    )(grads)


def project_kernel(
    sc_ref, tok_ref, wk_ref, wv_ref, e0, e1, e2, e3, o0, o1, o2, o3, wk_s, wv_s, sems
):
    copies = []
    for n in range(NDP):
        at = pl.ds(pl.multiple_of(lax.rem(sc_ref[5] + NDP - n, NDP) * FS, FS), FS)
        pair = (
            pltpu.make_async_copy(wk_ref.at[at], wk_s.at[n], sems.at[n, 0]),
            pltpu.make_async_copy(wv_ref.at[at], wv_s.at[n], sems.at[n, 1]),
        )
        for copy in pair:
            copy.start()
        copies.append(pair)
    xk, xv = [], []
    for h in range(KVH):
        base = (h // 2) * 8 + (h % 2) * 2
        total = tok_ref[base].astype(f32) + tok_ref[base + 1].astype(f32)
        total = total + tok_ref[base + 4].astype(f32) + tok_ref[base + 5].astype(f32)
        total = total.astype(bf16)
        xk.append(total[:, :HD])
        xv.append(total[:, HD:])
    xk, xv = jnp.concatenate(xk, 1), jnp.concatenate(xv, 1)
    token = lax.broadcasted_iota(jnp.int32, (SLOTS, FS), 0) * 32 + sc_ref[4]
    visible = token < sc_ref[3]
    sq = jnp.zeros((SLOTS, 1), f32)
    cross = jnp.zeros((SLOTS, 1), f32)
    outs = (o0, o1, o2, o3)
    for n, embed_ref in enumerate((e0, e1, e2, e3)):
        rows = embed_ref[:SLOTS, :].astype(f32)
        tail = embed_ref[SLOTS:, :].astype(f32)
        scale = tail[0:1] + tail[1:2] + tail[2:3]
        sq += jnp.sum(rows * rows, 1, keepdims=True)
        for copy in copies[n]:
            copy.wait()
        projected = mm(xk, wk_s[n], NT) + mm(xv, wv_s[n], NT)
        grad = jnp.where(visible, projected, 0.0).astype(bf16)
        outs[n][:, :FS] = grad
        cross += jnp.sum(rows * (scale * grad.astype(f32)), 1, keepdims=True)
    lane = lax.broadcasted_iota(jnp.int32, (SLOTS, 128), 1)
    parts = split3(lax.rsqrt(sq / D + norm_eps)) + split3(cross / D)
    tail = jnp.zeros((SLOTS, 128), f32)
    for n, part in enumerate(parts):
        tail = jnp.where(lane == n, part.astype(f32), tail)
    for n in range(NDP):
        outs[n][:, FS:] = tail.astype(bf16)


def project(sc, tok, wk, wv, embeds):
    one = jax.ShapeDtypeStruct((SLOTS, FS + 128), bf16)
    return pl.pallas_call(
        project_kernel,
        out_shape=(one,) * NDP,
        in_specs=[SM, VM, ANY, ANY] + [VM] * 4,
        out_specs=(VM,) * NDP,
        scratch_shapes=[
            pltpu.VMEM((NDP, FS, KVH * HD), bf16),
            pltpu.VMEM((NDP, FS, KVH * HD), bf16),
            pltpu.SemaphoreType.DMA((NDP, 2)),
        ],
        compiler_params=params(60),
        cost_estimate=cost(10),
        name="project",
    )(sc, tok, wk, wv, *embeds)


def norm_kernel(sc_ref, r0, r1, r2, r3, embed_ref, scale_ref, out_ref):
    lane = lax.broadcasted_iota(jnp.int32, (SLOTS, 128), 1)
    scale = scale_ref[...].reshape(1, FS)
    for n, recv_ref in enumerate((r0, r1, r2, r3)):
        row = sc_ref[n]
        tail = recv_ref[:, FS:].astype(f32)
        inv = jnp.sum(jnp.where(lane < 3, tail, 0.0), 1, keepdims=True)
        cross = jnp.sum(jnp.where(lane >= 3, tail, 0.0), 1, keepdims=True)
        scaled = scale * recv_ref[:, :FS].astype(f32)
        rows = embed_ref[row].astype(f32)
        out_ref[row] = inv * scaled - rows * (inv * inv * inv * cross)


def norm_grads(sc, recvs, embed, scale):
    return pl.pallas_call(
        norm_kernel,
        out_shape=jax.ShapeDtypeStruct((NDP, SLOTS, FS), f32),
        in_specs=[SM] + [VM] * 6,
        out_specs=VM,
        compiler_params=params(8),
        cost_estimate=cost(3),
        name="norm_grads",
    )(sc, *recvs, embed, scale)


def exchange(x, axes):
    return lax.all_to_all(x, axes, split_axis=0, concat_axis=0, tiled=True)


def shift(x, by):
    return lax.ppermute(x, "dp", [(i, (i + by) % NDP) for i in range(NDP)])


def swap(x, axis):
    return lax.ppermute(x, axis, [(0, 1), (1, 0)])


def local(
    query_states,
    key_states,
    value_states,
    out_grads,
    image_counts,
    prefix_lengths,
    encoder_owner,
    key_weight,
    value_weight,
    norm_scale,
    image_embed,
):
    ctx = ("y", "zh", "zl", "core")
    dp = lax.axis_index("dp")
    sc = jnp.stack(
        [
            prefix_lengths[0],
            lax.axis_index("zh"),
            lax.axis_index("core"),
            image_counts[0],
            lax.axis_index(ctx),
            dp,
        ]
    ).astype(jnp.int32)
    owner = lax.dynamic_slice(jnp.concatenate([encoder_owner, encoder_owner]), (dp,), (NDP,))

    kv0 = exchange(pack_heads(key_states[0], value_states[0], "pack_kv"), ("y", "zl"))
    kv1 = swap(kv0, "core")
    kv2 = swap(kv0, "zh")
    kv3 = swap(kv2, "core")
    qd = exchange(pack_heads(query_states[0], out_grads[0], "pack_qd"), ("y", "zl"))

    dq, own, core_part, far, farcore, tok = attention(sc, qd, kv0, kv1, kv2, kv3)

    packed = pack_embed(owner, image_embed, norm_scale)
    embeds = [packed[0]] + [shift(packed[n], n) for n in range(1, NDP)]
    tok_in = exchange(tok, ctx)
    far_sum = pair_sum(far, swap(farcore, "core"))
    payload = project(sc, tok_in, key_weight, value_weight, embeds)
    grads = last_sum(dq, own, swap(core_part, "core"), swap(far_sum, "zh"), payload[0])
    recvs = [payload[0]] + [shift(payload[n], -n) for n in range(1, NDP)]
    image_grads = norm_grads(owner, recvs, image_embed, norm_scale)
    query_grads, key_grads, value_grads = unpack(exchange(grads, ("y", "zl")))
    return (query_grads[None], key_grads[None], value_grads[None], image_grads)


def solution(mesh):
    ctx = ("y", "zh", "zl", "core")
    split = Mesh(mesh.devices.reshape(4, 4, 2, 2, 2), ("dp",) + ctx)
    rows = P("dp", ctx, None)
    image = P(None, ctx, "dp")
    in_specs = (rows, rows, rows, rows, P("dp"), P("dp"), P(), P(), P(), P("dp"), image)
    out_specs = (rows, rows, rows, image)
    return jax.shard_map(local, mesh=split, in_specs=in_specs, out_specs=out_specs, check_vma=False)
```

time: 171 us -> 140 us (0.82); the launches traced: 169 us -> 140 us
  waiting for transfers between devices: 43.6 us -> 28 us
  Pallas kernels: 62.5 us -> 54.1 us
  local copies, waits for them, and re-layouts: 12 us -> 6.08 us
    all_to_all x6 -> x3, waiting for transfers between devices: 29.1 us -> 1.92 us  [exchange(): return lax.all_to_all(x, axes, split_axis=0, concat_axis=0, tiled=True)]
    all_to_all x6 -> x3, starting transfers between devices: 26.7 us -> 13.7 us  [exchange(): return lax.all_to_all(x, axes, split_axis=0, concat_axis=0, tiled=True)]
    ppermute x0 -> x6, starting transfers between devices: none -> 12.5 us  [shift(): return lax.ppermute(x, 'dp', [(i, (i + by) % NDP) for i in range(NDP)])]
    ppermute x0 -> x6, waiting for transfers between devices: none -> 11.5 us  [shift(): return lax.ppermute(x, 'dp', [(i, (i + by) % NDP) for i in range(NDP)])]
    unnamed x24 -> x32, local copies, waits for them, and re-layouts: 10.7 us -> 5.34 us
    pallas_call x1, Pallas kernels: 4.37 us -> 1.86 us  [norm_grads(): pl.pallas_call(norm_kernel, out_shape=jax.ShapeDtypeStruct((NDP, SLOTS, F...]
    pallas_call x1, Pallas kernels: 2.12 us -> 0.14 us  [pair_sum(): pl.pallas_call(pair_sum_kernel, out_shape=jax.ShapeDtypeStruct(a.shape, b...]
    pallas_call x1, Pallas kernels: 35 us -> 33 us  [attention(): pl.pallas_call(attention_kernel, out_shape=(jax.ShapeDtypeStruct(part, bf...]
  transfers between devices with their start and end apart: 12 -> 15, of which waited for: 4 -> 7; matrix products, arithmetic and copies ran while one was open for 1% -> 1% of each run, Pallas kernels for 34% -> 12%
where the time goes in v2:
time: 140 us
  Pallas kernels  54.1 us (39%)
  starting transfers between devices  33.9 us (24%)
  waiting for transfers between devices  28 us (20%)
  blocking collectives  15.6 us (11%)
  local copies, waits for them, and re-layouts  6.08 us (4%)
  between operations  2.09 us (1%)
    pallas_call x1, Pallas kernels, attention(): pl.pallas_call(attention_kernel, out_shape=(jax.ShapeDtypeStruct(part, bf...  33 us
    all_to_all x1, blocking collectives, exchange(): return lax.all_to_all(x, axes, split_axis=0, concat_axis=0, tiled=True)  15.6 us
    ppermute x6, waiting for transfers between devices, swap(): return lax.ppermute(x, axis, [(0, 1), (1, 0)])  14.5 us
    all_to_all x3, starting transfers between devices, exchange(): return lax.all_to_all(x, axes, split_axis=0, concat_axis=0, tiled=True)  13.7 us
    ppermute x6, starting transfers between devices, shift(): return lax.ppermute(x, 'dp', [(i, (i + by) % NDP) for i in range(NDP)])  12.5 us
    pallas_call x1, Pallas kernels, project(): pl.pallas_call(project_kernel, out_shape=(one,) * NDP, in_specs=[SM, VM,...  11.9 us
    ppermute x6, waiting for transfers between devices, shift(): return lax.ppermute(x, 'dp', [(i, (i + by) % NDP) for i in range(NDP)])  11.5 us
    ppermute x6, starting transfers between devices, swap(): return lax.ppermute(x, axis, [(0, 1), (1, 0)])  7.72 us
  transfers between devices with their start and end apart: 15, of which 7 were waited for; matrix products, arithmetic and copies ran while one was open for 1% of the time, Pallas kernels for 12%

profile of v2, /device:TPU:0, one launch (start us, length us, event | category | flops | bytes accessed | tf_op | source)
XLA Modules:
  0.0 139.8 jit_solution(4660665813876123919)
XLA Ops:
  0.7 2.0 %pack_kv.1 = bf16[8,128,256]{2,1,0:T(8,128)(2,1)} custom-call(bf16[128,1024]{1,0:T(8,128)(2,1)} %bitcast.13, bf16[128,1024]{1,0:T(8,128)(2,1)} %bitcast.14), custom_call_target="tpu_custom_call" | custom-call | bytes 6000000 | tf_op jit(solution)/shard_map/pack_kv/pallas_call | solution.py:64
  2.6 15.6 %all_to_all.20.kv0_ref = bf16[8,128,256]{2,1,0:T(8,128)(2,1)S(1)} all-to-all(bf16[8,128,256]{2,1,0:T(8,128)(2,1)} %pack_kv.1), channel_id=1, replica_groups=mesh['dp'=4,'y'=4,'zh'=2,'zl'=2,'core'=2] {'y','zl'}, dimensions={0} | all-to-all | bytes 1048576 | tf_op jit(solution)/shard_map/all_to_all | solution.py:429
  18.3 3.6 %collective-permute-start.1 = (bf16[8,128,256]{2,1,0:T(8,128)(2,1)S(1)}, bf16[8,128,256]{2,1,0:T(8,128)(2,1)S(1)}, u32[]{:S(2)}, u32[]{:S(2)}) collective-permute-start(bf16[8,128,256]{2,1,0:T(8,128)(2,1)S(1)} %all_to_all.20.kv0_ref), channel_id=1, source_target_pairs={{0,4},{4,0},{1,5},{5,1},{2,6},{6,2},{3,7},{7,3},{8,12},{12,8},{9,1... | collective-permute-start | bytes 1572872 | tf_op jit(solution)/shard_map/ppermute | solution.py:437
  21.9 2.3 %pack_qd.1 = bf16[8,128,512]{2,1,0:T(8,128)(2,1)} custom-call(bf16[128,2048]{1,0:T(8,128)(2,1)} %bitcast.11, bf16[128,2048]{1,0:T(8,128)(2,1)} %bitcast.12), custom_call_target="tpu_custom_call" | custom-call | bytes 6000000 | tf_op jit(solution)/shard_map/pack_qd/pallas_call | solution.py:64
  24.1 3.6 %all-to-all-start = ((bf16[8,128,512]{2,1,0:T(8,128)(2,1)}), bf16[8,128,512]{2,1,0:T(8,128)(2,1)S(1)}, u32[]{:S(2)}, u32[]{:S(2)}) async-start(bf16[8,128,512]{2,1,0:T(8,128)(2,1)} %pack_qd.1), calls=%async_computation | async-start | bytes 2097152 | tf_op jit(solution)/shard_map/all_to_all | solution.py:429
  27.8 14.4 %collective-permute-done.1.kv2_ref = bf16[8,128,256]{2,1,0:T(8,128)(2,1)S(1)} collective-permute-done((bf16[8,128,256]{2,1,0:T(8,128)(2,1)S(1)}, bf16[8,128,256]{2,1,0:T(8,128)(2,1)S(1)}, u32[]{:S(2)}, u32[]{:S(2)}) %collective-permute-start.1) | collective-permute-done | bytes 524320 | tf_op jit(solution)/shard_map/ppermute | solution.py:437
  45.3 33.0 %attention.1 = (bf16[8,128,256]{2,1,0:T(8,128)(2,1)}, f32[8,128,256]{2,1,0:T(8,128)}, bf16[8,128,256]{2,1,0:T(8,128)(2,1)}, bf16[8,128,256]{2,1,0:T(8,128)(2,1)}...) custom-call(s32[6]{0:T(128)} %stack.19.sc_ref, bf16[8,128,512]{2,1,0:T(8,128)(2,1)} %copy-done.8, ...), custom_call_target="tpu_custom_call" | custom-call | bytes 108000000 | tf_op jit(solution)/shard_map/attention/pallas_call | solution.py:246
  78.8 5.8 %all-to-all-start.2 = ((bf16[32,64,256]{2,1,0:T(8,128)(2,1)}), bf16[32,64,256]{2,1,0:T(8,128)(2,1)}, u32[]{:S(2)}, u32[]{:S(2)}) async-start(bf16[32,64,256]{2,1,0:T(8,128)(2,1)} %get-tuple-element.26), calls=%async_computation.2 | async-start | bytes 2097152 | tf_op jit(solution)/shard_map/all_to_all | solution.py:429
  85.0 1.0 copy-done.4
  86.1 3.3 %collective-permute-start.5 = (bf16[8,128,256]{2,1,0:T(8,128)(2,1)S(1)}, bf16[8,128,256]{2,1,0:T(8,128)(2,1)S(1)}, u32[]{:S(2)}, u32[]{:S(2)}) collective-permute-start(bf16[8,128,256]{2,1,0:T(8,128)(2,1)S(1)} %pair_sum.1), channel_id=1, source_target_pairs={{0,4},{4,0},{1,5},{5,1},{2,6},{6,2},{3,7},{7,3},{8,12},{12,8},{9,1... | collective-permute-start | bytes 1572872 | tf_op jit(solution)/shard_map/ppermute | solution.py:437
  90.8 5.2 %collective-permute-start.7 = (bf16[80,1152]{1,0:T(8,128)(2,1)S(1)}, bf16[80,1152]{1,0:T(8,128)(2,1)S(1)}, u32[]{:S(2)}, u32[]{:S(2)}) collective-permute-start(bf16[80,1152]{1,0:T(8,128)(2,1)S(1)} %get-tuple-element.29), channel_id=1, source_target_pairs={{0,64},{32,96},{64,0},{96,32},{1,65},{33,97},{65,1},{97,33},{2,66}... | collective-permute-start | bytes 552968 | tf_op jit(solution)/shard_map/ppermute | solution.py:433
  96.1 1.4 %collective-permute-start.8 = (bf16[80,1152]{1,0:T(8,128)(2,1)S(1)}, bf16[80,1152]{1,0:T(8,128)(2,1)S(1)}, u32[]{:S(2)}, u32[]{:S(2)}) collective-permute-start(bf16[80,1152]{1,0:T(8,128)(2,1)S(1)} %get-tuple-element.30), channel_id=1, source_target_pairs={{0,96},{32,0},{64,32},{96,64},{1,97},{33,1},{65,33},{97,65},{2,98}... | collective-permute-start | bytes 552968 | tf_op jit(solution)/shard_map/ppermute | solution.py:433
  97.5 2.0 %collective-permute-done.6.e1 = bf16[80,1152]{1,0:T(8,128)(2,1)S(1)} collective-permute-done((bf16[80,1152]{1,0:T(8,128)(2,1)S(1)}, bf16[80,1152]{1,0:T(8,128)(2,1)S(1)}, u32[]{:S(2)}, u32[]{:S(2)}) %collective-permute-start.6) | collective-permute-done | bytes 184352 | tf_op jit(solution)/shard_map/ppermute | solution.py:433
  99.5 5.1 %collective-permute-done.7.e2 = bf16[80,1152]{1,0:T(8,128)(2,1)S(1)} collective-permute-done((bf16[80,1152]{1,0:T(8,128)(2,1)S(1)}, bf16[80,1152]{1,0:T(8,128)(2,1)S(1)}, u32[]{:S(2)}, u32[]{:S(2)}) %collective-permute-start.7) | collective-permute-done | bytes 184352 | tf_op jit(solution)/shard_map/ppermute | solution.py:433
  105.3 11.9 %project.1 = (bf16[64,1280]{1,0:T(8,128)(2,1)}, bf16[64,1280]{1,0:T(8,128)(2,1)}, bf16[64,1280]{1,0:T(8,128)(2,1)}, bf16[64,1280]{1,0:T(8,128)(2,1)}) custom-call(s32[6]{0:T(128)} %stack.19.sc_ref, bf16[32,64,256]{2,1,0:T(8,128)(2,1)} %all-to-all-done.2.tok_ref, bf16[4608,1024]{1,0:T(8,128)(2,1)} %wk_ref.1, bf16[4608,1024]{1,0:T(8,128)(2,1)} %wv_ref.1, ...), custom_call_target="tpu_custom_call" | custom-call | bytes 30000000 | tf_op jit(solution)/shard_map/project/pallas_call | solution.py:387
  118.2 1.2 last_sum.1
  119.4 4.3 %all-to-all-start.3 = ((bf16[8,128,512]{2,1,0:T(8,128)(2,1)}), bf16[8,128,512]{2,1,0:T(8,128)(2,1)S(1)}, u32[]{:S(2)}, u32[]{:S(2)}) async-start(bf16[8,128,512]{2,1,0:T(8,128)(2,1)} %last_sum.1), calls=%async_computation.3 | async-start | bytes 2097152 | tf_op jit(solution)/shard_map/all_to_all | solution.py:429
  123.7 2.6 %collective-permute-start.10 = (bf16[64,1280]{1,0:T(8,128)(2,1)}, bf16[64,1280]{1,0:T(8,128)(2,1)S(1)}, u32[]{:S(2)}, u32[]{:S(2)}) collective-permute-start(bf16[64,1280]{1,0:T(8,128)(2,1)} %get-tuple-element.36), channel_id=1, source_target_pairs={{0,64},{32,96},{64,0},{96,32},{1,65},{33,97},{65,1},{97,33},{2,66}... | collective-permute-start | bytes 491528 | tf_op jit(solution)/shard_map/ppermute | solution.py:433
  126.6 3.0 %collective-permute-start.9 = (bf16[64,1280]{1,0:T(8,128)(2,1)}, bf16[64,1280]{1,0:T(8,128)(2,1)S(1)}, u32[]{:S(2)}, u32[]{:S(2)}) collective-permute-start(bf16[64,1280]{1,0:T(8,128)(2,1)} %get-tuple-element.35), channel_id=1, source_target_pairs={{0,96},{32,0},{64,32},{96,64},{1,97},{33,1},{65,33},{97,65},{2,98}... | collective-permute-start | bytes 491528 | tf_op jit(solution)/shard_map/ppermute | solution.py:433
  129.5 2.8 %collective-permute-done.10.r2 = bf16[64,1280]{1,0:T(8,128)(2,1)S(1)} collective-permute-done((bf16[64,1280]{1,0:T(8,128)(2,1)}, bf16[64,1280]{1,0:T(8,128)(2,1)S(1)}, u32[]{:S(2)}, u32[]{:S(2)}) %collective-permute-start.10) | collective-permute-done | bytes 163872 | tf_op jit(solution)/shard_map/ppermute | solution.py:433
  132.3 1.7 %collective-permute-done.11.r3 = bf16[64,1280]{1,0:T(8,128)(2,1)S(1)} collective-permute-done((bf16[64,1280]{1,0:T(8,128)(2,1)}, bf16[64,1280]{1,0:T(8,128)(2,1)S(1)}, u32[]{:S(2)}, u32[]{:S(2)}) %collective-permute-start.11) | collective-permute-done | bytes 163872 | tf_op jit(solution)/shard_map/ppermute | solution.py:433
  134.9 1.9 %norm_grads.1 = f32[4,64,1152]{2,1,0:T(8,128)} custom-call(s32[4]{0:T(128)S(1)} %dynamic_slice.3.sc_ref, bf16[64,1280]{1,0:T(8,128)(2,1)S(1)} %copy-done.3, bf16[64,1280]{1,0:T(8,128)(2,1)S(1)} %collective-permute-done.9.r1, bf16[64,1280]{1,0:T(8,128)(2,1)S(1)} %collective-permute-done.10.r2, bf16[64,1280]{1,0:T(8,128)(2,1)S(1)} %collective-permute-done.11.r3, ...), custom_call_target="tpu_custom_call" | custom-call | bytes 9000000 | tf_op jit(solution)/shard_map/norm_grads/pallas_call | solution.py:417
  136.8 1.9 %all-to-all-done.3.in_ref = bf16[8,128,512]{2,1,0:T(8,128)(2,1)S(1)} async-done(((bf16[8,128,512]{2,1,0:T(8,128)(2,1)}), bf16[8,128,512]{2,1,0:T(8,128)(2,1)S(1)}, u32[]{:S(2)}, u32[]{:S(2)}) %all-to-all-start.3) | async-done | bytes 1048608 | tf_op jit(solution)/shard_map/all_to_all | solution.py:429
  138.7 1.2 unpack.1
  (51 shorter events, 7.1 us)
Async XLA Ops:
  0.6 88.8 %copy-start.15 = (s32[4]{0:T(128)S(1)}, s32[4]{0:T(128)}, u32[]{:S(2)}) copy-start(s32[4]{0:T(128)} %param.17) | copy-start | bytes 52
  0.6 88.9 %copy-start.7 = (f32[1152]{0:T(1024)S(1)}, f32[1152]{0:T(1024)}, u32[]{:S(2)}) copy-start(f32[1152]{0:T(1024)} %scale_ref.3) | copy-start | bytes 13828
  0.7 88.9 %copy-start = (bf16[4,64,1152]{2,1,0:T(8,128)(2,1)S(1)}, bf16[4,64,1152]{2,1,0:T(8,128)(2,1)}, u32[]{:S(2)}) copy-start(bf16[4,64,1152]{2,1,0:T(8,128)(2,1)} %embed_ref.3) | copy-start | bytes 1769476
  18.3 26.0 %copy-start.9 = (bf16[8,128,256]{2,1,0:T(8,128)(2,1)}, bf16[8,128,256]{2,1,0:T(8,128)(2,1)S(1)}, u32[]{:S(2)}) copy-start(bf16[8,128,256]{2,1,0:T(8,128)(2,1)S(1)} %all_to_all.20.kv0_ref) | copy-start | bytes 1572868
  18.3 23.9 %collective-permute-start.1 = (bf16[8,128,256]{2,1,0:T(8,128)(2,1)S(1)}, bf16[8,128,256]{2,1,0:T(8,128)(2,1)S(1)}, u32[]{:S(2)}, u32[]{:S(2)}) collective-permute-start(bf16[8,128,256]{2,1,0:T(8,128)(2,1)S(1)} %all_to_all.20.kv0_ref), channel_id=1, source_target_pairs={{0,4},{4,0},{1,5},{5,1},{2,6},{6,2},{3,7},{7,3},{8,12},{12,8},{9,1... | collective-permute-start | bytes 1572872 | tf_op jit(solution)/shard_map/ppermute | solution.py:437
  24.1 20.1 %all-to-all-start = ((bf16[8,128,512]{2,1,0:T(8,128)(2,1)}), bf16[8,128,512]{2,1,0:T(8,128)(2,1)S(1)}, u32[]{:S(2)}, u32[]{:S(2)}) async-start(bf16[8,128,512]{2,1,0:T(8,128)(2,1)} %pack_qd.1), calls=%async_computation | async-start | bytes 2097152 | tf_op jit(solution)/shard_map/all_to_all | solution.py:429
  27.7 16.5 %collective-permute-start = (bf16[8,128,256]{2,1,0:T(8,128)(2,1)S(1)}, bf16[8,128,256]{2,1,0:T(8,128)(2,1)S(1)}, u32[]{:S(2)}, u32[]{:S(2)}) collective-permute-start(bf16[8,128,256]{2,1,0:T(8,128)(2,1)S(1)} %all_to_all.20.kv0_ref), channel_id=1, source_target_pairs={{0,1},{1,0},{2,3},{3,2},{4,5},{5,4},{6,7},{7,6},{8,9},{9,8},{10,11... | collective-permute-start | bytes 1572872 | tf_op jit(solution)/shard_map/ppermute | solution.py:437
  42.2 2.0 %copy-start.10 = (bf16[8,128,256]{2,1,0:T(8,128)(2,1)}, bf16[8,128,256]{2,1,0:T(8,128)(2,1)S(1)}, u32[]{:S(2)}) copy-start(bf16[8,128,256]{2,1,0:T(8,128)(2,1)S(1)} %collective-permute-done.1.kv2_ref) | copy-start | bytes 1572868
  42.2 2.0 %collective-permute-start.2 = (bf16[8,128,256]{2,1,0:T(8,128)(2,1)S(1)}, bf16[8,128,256]{2,1,0:T(8,128)(2,1)}, u32[]{:S(2)}, u32[]{:S(2)}) collective-permute-start(bf16[8,128,256]{2,1,0:T(8,128)(2,1)S(1)} %collective-permute-done.1.kv2_ref), channel_id=1, source_target_pairs={{0,1},{1,0},{2,3},{3,2},{4,5},{5,4},{6,7},{7,6},{8,9},{9,8},{10,11... | collective-permute-start | bytes 1572872 | tf_op jit(solution)/shard_map/ppermute | solution.py:437
  44.2 1.1 copy-start.11
  78.3 6.6 %collective-permute-start.4 = (bf16[8,128,256]{2,1,0:T(8,128)(2,1)}, bf16[8,128,256]{2,1,0:T(8,128)(2,1)S(1)}, u32[]{:S(2)}, u32[]{:S(2)}) collective-permute-start(bf16[8,128,256]{2,1,0:T(8,128)(2,1)} %get-tuple-element.25), channel_id=1, source_target_pairs={{0,1},{1,0},{2,3},{3,2},{4,5},{5,4},{6,7},{7,6},{8,9},{9,8},{10,11... | collective-permute-start | bytes 1572872 | tf_op jit(solution)/shard_map/ppermute | solution.py:437
  78.8 25.8 %all-to-all-start.2 = ((bf16[32,64,256]{2,1,0:T(8,128)(2,1)}), bf16[32,64,256]{2,1,0:T(8,128)(2,1)}, u32[]{:S(2)}, u32[]{:S(2)}) async-start(bf16[32,64,256]{2,1,0:T(8,128)(2,1)} %get-tuple-element.26), calls=%async_computation.2 | async-start | bytes 2097152 | tf_op jit(solution)/shard_map/all_to_all | solution.py:429
  84.7 32.6 %collective-permute-start.3 = (bf16[8,128,256]{2,1,0:T(8,128)(2,1)}, bf16[8,128,256]{2,1,0:T(8,128)(2,1)S(1)}, u32[]{:S(2)}, u32[]{:S(2)}) collective-permute-start(bf16[8,128,256]{2,1,0:T(8,128)(2,1)} %get-tuple-element.23), channel_id=1, source_target_pairs={{0,1},{1,0},{2,3},{3,2},{4,5},{5,4},{6,7},{7,6},{8,9},{9,8},{10,11... | collective-permute-start | bytes 1572872 | tf_op jit(solution)/shard_map/ppermute | solution.py:437
  86.1 31.1 %collective-permute-start.5 = (bf16[8,128,256]{2,1,0:T(8,128)(2,1)S(1)}, bf16[8,128,256]{2,1,0:T(8,128)(2,1)S(1)}, u32[]{:S(2)}, u32[]{:S(2)}) collective-permute-start(bf16[8,128,256]{2,1,0:T(8,128)(2,1)S(1)} %pair_sum.1), channel_id=1, source_target_pairs={{0,4},{4,0},{1,5},{5,1},{2,6},{6,2},{3,7},{7,3},{8,12},{12,8},{9,1... | collective-permute-start | bytes 1572872 | tf_op jit(solution)/shard_map/ppermute | solution.py:437
  90.8 8.6 %collective-permute-start.6 = (bf16[80,1152]{1,0:T(8,128)(2,1)S(1)}, bf16[80,1152]{1,0:T(8,128)(2,1)S(1)}, u32[]{:S(2)}, u32[]{:S(2)}) collective-permute-start(bf16[80,1152]{1,0:T(8,128)(2,1)S(1)} %get-tuple-element.28), channel_id=1, source_target_pairs={{0,32},{32,64},{64,96},{96,0},{1,33},{33,65},{65,97},{97,1},{2,34}... | collective-permute-start | bytes 552968 | tf_op jit(solution)/shard_map/ppermute | solution.py:433
  90.8 13.8 %collective-permute-start.7 = (bf16[80,1152]{1,0:T(8,128)(2,1)S(1)}, bf16[80,1152]{1,0:T(8,128)(2,1)S(1)}, u32[]{:S(2)}, u32[]{:S(2)}) collective-permute-start(bf16[80,1152]{1,0:T(8,128)(2,1)S(1)} %get-tuple-element.29), channel_id=1, source_target_pairs={{0,64},{32,96},{64,0},{96,32},{1,65},{33,97},{65,1},{97,33},{2,66}... | collective-permute-start | bytes 552968 | tf_op jit(solution)/shard_map/ppermute | solution.py:433
  96.1 8.5 %collective-permute-start.8 = (bf16[80,1152]{1,0:T(8,128)(2,1)S(1)}, bf16[80,1152]{1,0:T(8,128)(2,1)S(1)}, u32[]{:S(2)}, u32[]{:S(2)}) collective-permute-start(bf16[80,1152]{1,0:T(8,128)(2,1)S(1)} %get-tuple-element.30), channel_id=1, source_target_pairs={{0,96},{32,0},{64,32},{96,64},{1,97},{33,1},{65,33},{97,65},{2,98}... | collective-permute-start | bytes 552968 | tf_op jit(solution)/shard_map/ppermute | solution.py:433
  99.5 5.9 %copy-start.12 = (bf16[80,1152]{1,0:T(8,128)(2,1)}, bf16[80,1152]{1,0:T(8,128)(2,1)S(1)}, u32[]{:S(2)}) copy-start(bf16[80,1152]{1,0:T(8,128)(2,1)S(1)} %collective-permute-done.6.e1) | copy-start | bytes 552964
  105.3 12.0 %copy-start.1 = (f32[8,128,256]{2,1,0:T(8,128)S(1)}, f32[8,128,256]{2,1,0:T(8,128)}, u32[]{:S(2)}) copy-start(f32[8,128,256]{2,1,0:T(8,128)} %get-tuple-element.22.a_ref) | copy-start | bytes 3145732
  105.3 12.0 %copy-start.5 = (bf16[8,128,256]{2,1,0:T(8,128)(2,1)S(1)}, bf16[8,128,256]{2,1,0:T(8,128)(2,1)}, u32[]{:S(2)}) copy-start(bf16[8,128,256]{2,1,0:T(8,128)(2,1)} %get-tuple-element.21.dq_ref) | copy-start | bytes 1572868
  119.4 19.2 %all-to-all-start.3 = ((bf16[8,128,512]{2,1,0:T(8,128)(2,1)}), bf16[8,128,512]{2,1,0:T(8,128)(2,1)S(1)}, u32[]{:S(2)}, u32[]{:S(2)}) async-start(bf16[8,128,512]{2,1,0:T(8,128)(2,1)} %last_sum.1), calls=%async_computation.3 | async-start | bytes 2097152 | tf_op jit(solution)/shard_map/all_to_all | solution.py:429
  123.7 8.6 %collective-permute-start.10 = (bf16[64,1280]{1,0:T(8,128)(2,1)}, bf16[64,1280]{1,0:T(8,128)(2,1)S(1)}, u32[]{:S(2)}, u32[]{:S(2)}) collective-permute-start(bf16[64,1280]{1,0:T(8,128)(2,1)} %get-tuple-element.36), channel_id=1, source_target_pairs={{0,64},{32,96},{64,0},{96,32},{1,65},{33,97},{65,1},{97,33},{2,66}... | collective-permute-start | bytes 491528 | tf_op jit(solution)/shard_map/ppermute | solution.py:433
  126.3 7.7 %collective-permute-start.11 = (bf16[64,1280]{1,0:T(8,128)(2,1)}, bf16[64,1280]{1,0:T(8,128)(2,1)S(1)}, u32[]{:S(2)}, u32[]{:S(2)}) collective-permute-start(bf16[64,1280]{1,0:T(8,128)(2,1)} %get-tuple-element.37), channel_id=1, source_target_pairs={{0,32},{32,64},{64,96},{96,0},{1,33},{33,65},{65,97},{97,1},{2,34}... | collective-permute-start | bytes 491528 | tf_op jit(solution)/shard_map/ppermute | solution.py:433
  126.6 7.4 %collective-permute-start.9 = (bf16[64,1280]{1,0:T(8,128)(2,1)}, bf16[64,1280]{1,0:T(8,128)(2,1)S(1)}, u32[]{:S(2)}, u32[]{:S(2)}) collective-permute-start(bf16[64,1280]{1,0:T(8,128)(2,1)} %get-tuple-element.35), channel_id=1, source_target_pairs={{0,96},{32,0},{64,32},{96,64},{1,97},{33,1},{65,33},{97,65},{2,98}... | collective-permute-start | bytes 491528 | tf_op jit(solution)/shard_map/ppermute | solution.py:433
  (7 other events, 5.9 us)
